TPU v7x, 256 devices: a whole 4x4x8 slice. The times are simulated.
256 devices in a mesh: quad: 8 (over z_lo, core), dom: 32 (over x, y, z_hi).
Axes of the slice: x: 4, y: 4, z: 8 (z_hi: 2, z_lo: 4; z = z_hi * 4 + z_lo), core: 2. Of those that a mesh axis runs over, the one named last changes fastest.
Arguments:
- probes: float32 [2, 64, 256, 128], P(None, None, 'dom'), may hold values from -6 to 6
- mass_weights: float32 [256, 128], P('dom'), may hold values from 0.8 to 1.25
- blocks: float32 [2, 256, 128, 128], P(None, 'dom'), may hold values from -4 to 4
- couplings: float32 [2, 6, 256, 128], P(None, None, 'dom'), may hold values from -0.25 to 0.25
Outputs:
- moments: float32 [64, 4, 2, 256, 128], P('quad', None, None, 'dom')
- projected: float32 [2, 8, 64, 64], replicated
All inputs are finite; a program needn't handle non-finite values.
Results may differ from a plain program's by a relative error of at most 0.0001.
Values sent between devices are 32-bit elements; how exact they have to be, the bound alone decides.
A program may use at most 64 MiB of HBM per device.

v0:
```python
import math

import jax
import jax.numpy as jnp
from jax import lax
from jax.sharding import PartitionSpec as P

NQ = 16
ITERS = 4
MOM = 4


PRECISE = lax.Precision.HIGHEST
RADIUS = 2.0
OFFSETS = (-3, -2, -1, 1, 2, 3)


def with_halo(cells, sides, width):
    for axis, dim in sides:
        count = lax.axis_size(axis)
        ends = count - 1
        head = lax.slice_in_dim(cells, 0, width, axis=dim)
        tail = lax.slice_in_dim(cells, cells.shape[dim] - width, cells.shape[dim], axis=dim)
        cells = jnp.concatenate(
            [
                lax.ppermute(tail, axis, [(i, (i + 1) % count) for i in range(ends)]),
                cells,
                lax.ppermute(head, axis, [((i + 1) % count, i) for i in range(ends)]),
            ],
            axis=dim,
        )
    return cells


def shift_angles(shift_index, total_shifts):
    return 2.0 * math.pi / total_shifts * (shift_index.astype(jnp.float32) + 0.5)


def moment_weights(angles, moment_count, scale):
    orders = jnp.arange(1, moment_count + 1, dtype=jnp.float32)
    phases = orders[:, None] * angles[None, :]
    return (scale * jnp.cos(phases), scale * jnp.sin(phases))


def sweep(field, padded, blocks, couplings, zmass_re, zmass_im, inverse_re, inverse_im, source):
    rim_depth = max(OFFSETS)
    line_count = field.shape[3]
    field_re = field[0]
    field_im = field[1]
    image_re = jnp.einsum("spxj,xij->spxi", field_re, blocks[0], precision=PRECISE) - jnp.einsum(
        "spxj,xij->spxi", field_im, blocks[1], precision=PRECISE
    )
    image_im = jnp.einsum("spxj,xij->spxi", field_im, blocks[0], precision=PRECISE) + jnp.einsum(
        "spxj,xij->spxi", field_re, blocks[1], precision=PRECISE
    )
    for position, offset in enumerate(OFFSETS):
        neighbour = padded[:, :, :, rim_depth + offset : rim_depth + offset + line_count]
        coup_re = couplings[0, position]
        coup_im = couplings[1, position]
        image_re = image_re + coup_re * neighbour[0] - coup_im * neighbour[1]
        image_im = image_im + coup_re * neighbour[1] + coup_im * neighbour[0]
    resid_re = source[0] - (zmass_re * field_re - zmass_im * field_im) + image_re
    resid_im = source[1] - (zmass_re * field_im + zmass_im * field_re) + image_im
    return jnp.stack(
        [
            field_re + resid_re * inverse_re - resid_im * inverse_im,
            field_im + resid_re * inverse_im + resid_im * inverse_re,
        ]
    )


def moment_block(field_part, weight_re, weight_im):
    sum_re = jnp.einsum("ks,spxi->pkxi", weight_re, field_part[0], precision=PRECISE) - jnp.einsum(
        "ks,spxi->pkxi", weight_im, field_part[1], precision=PRECISE
    )
    sum_im = jnp.einsum("ks,spxi->pkxi", weight_re, field_part[1], precision=PRECISE) + jnp.einsum(
        "ks,spxi->pkxi", weight_im, field_part[0], precision=PRECISE
    )
    return jnp.stack([sum_re, sum_im], axis=2)


def project(gram_re, gram_im, angles, scale):
    proj_re, proj_im = moment_weights(angles, 2 * MOM, scale)
    mixed_re = jnp.einsum("ks,spq->kpq", proj_re, gram_re, precision=PRECISE) - jnp.einsum(
        "ks,spq->kpq", proj_im, gram_im, precision=PRECISE
    )
    mixed_im = jnp.einsum("ks,spq->kpq", proj_re, gram_im, precision=PRECISE) + jnp.einsum(
        "ks,spq->kpq", proj_im, gram_re, precision=PRECISE
    )
    return jnp.stack([mixed_re, mixed_im])


def on_device(probes, mass_weights, blocks, couplings):
    rim_depth = max(OFFSETS)
    shift_count = NQ // lax.axis_size("quad")
    probe_count = probes.shape[1]
    owned_probes = probe_count // lax.axis_size("quad")
    line_count = probes.shape[2]
    row_width = probes.shape[3]
    total_lines = line_count * lax.axis_size("dom")
    shift_index = lax.axis_index("quad") * shift_count + jnp.arange(shift_count, dtype=jnp.int32)
    angles = shift_angles(shift_index, NQ)
    zmass_re = (RADIUS * jnp.cos(angles))[:, None, None, None] * mass_weights[None, None]
    zmass_im = (RADIUS * jnp.sin(angles))[:, None, None, None] * mass_weights[None, None]
    diagonal = jnp.diagonal(blocks, axis1=2, axis2=3)
    denom_re = zmass_re - diagonal[0]
    denom_im = zmass_im - diagonal[1]
    modulus = denom_re * denom_re + denom_im * denom_im
    inverse_re = denom_re / modulus
    inverse_im = -denom_im / modulus
    source = mass_weights[None, None] * probes
    field = jnp.stack(
        [
            source[0] * inverse_re - source[1] * inverse_im,
            source[0] * inverse_im + source[1] * inverse_re,
        ]
    )
    for step in range(ITERS - 1):
        padded = with_halo(field, (("dom", 3),), rim_depth)
        field = sweep(
            field, padded, blocks, couplings, zmass_re, zmass_im, inverse_re, inverse_im, source
        )
    weight_re, weight_im = moment_weights(angles, MOM, RADIUS / NQ)
    field_rows = lax.slice_in_dim(field, 0, owned_probes * lax.axis_size("quad"), axis=2)
    moments = lax.psum_scatter(
        moment_block(field_rows, weight_re, weight_im), "quad", scatter_dimension=0, tiled=True
    )
    gram_re = jnp.einsum("pxi,sqxi->spq", probes[0], field[0], precision=PRECISE) + jnp.einsum(
        "pxi,sqxi->spq", probes[1], field[1], precision=PRECISE
    )
    gram_im = jnp.einsum("pxi,sqxi->spq", probes[0], field[1], precision=PRECISE) - jnp.einsum(
        "pxi,sqxi->spq", probes[1], field[0], precision=PRECISE
    )
    scale = RADIUS / (NQ * total_lines * row_width)
    projected = lax.psum(project(gram_re, gram_im, angles, scale), ("quad", "dom"))
    return (moments, projected)


def solution(mesh):
    return jax.shard_map(
        on_device,
        mesh=mesh,
        in_specs=(
            P(None, None, "dom", None),
            P("dom", None),
            P(None, "dom", None, None),
            P(None, None, "dom", None),
        ),
        out_specs=(P("quad", None, None, "dom", None), P()),
        check_vma=False,
    )
```

profile of v0, /device:TPU:1, one launch (start us, length us, event | category | flops | bytes accessed | tf_op | source)
XLA Modules:
  0.0 444.3 jit_solution(10704677841827037540)
XLA Ops:
  8.0 0.0 all-reduce.2.cloned.1.call-start
  8.1 0.0 copy-start.1
  8.1 0.0 copy-start.3
  8.1 13.3 %copy.50 = f32[2,8,128,128]{1,0,3,2:T(2,128)} copy(f32[2,8,128,128]{3,2,1,0:T(8,128)} %param.6) | data formatting | bytes 2097152 | tf_op args[2]
  21.3 6.7 %gather_fusion = f32[128,2,8]{2,1,0:T(2,128)S(1)} fusion(f32[2,8,128,128]{1,0,3,2:T(2,128)} %copy.50, s32[128]{0:T(128)S(1)} %or_bitcast_fusion), kind=kCustom, calls=%fused_computation | custom fusion | bytes 17408 | tf_op jit(solution)/shard_map/jit(diagonal)/gather | solution.py:105
  28.0 0.1 fusion.130
  28.2 0.1 copy.51
  28.3 0.1 sine_multiply_fusion
  28.4 0.1 copy.53
  28.5 0.1 copy.49
  28.6 0.1 fusion.78
  28.7 0.2 multiply_subtract_fusion.3
  28.8 0.1 pad_maximum_fusion.9
  28.9 1.4 collective-permute-start.1
  30.4 10.3 %collective-permute-start = (f32[2,2,64,3,128]{4,2,1,3,0:T(8,128)S(1)}, f32[2,2,64,3,128]{4,2,1,3,0:T(8,128)S(1)}, u32[]{:S(2)}, u32[]{:S(2)}) collective-permute-start(f32[2,2,64,3,128]{4,2,1,3,0:T(8,128)S(1)} %get-tuple-element.25), channel_id=1, source_target_pairs={{0,1},{1,2},{2,3},{3,4},{4,5},{5,6},{6,7},{7,8},{8,9},{9,10},{10,1... | collective-permute-start | bytes 1179656 | tf_op jit(solution)/shard_map/ppermute | solution.py:26
  40.7 1.2 fusion.30
  42.0 1.2 fusion.28
  43.2 4.5 %collective-permute-done.1 = f32[2,2,64,3,128]{4,2,1,3,0:T(8,128)S(1)} collective-permute-done((f32[2,2,64,3,128]{4,2,1,3,0:T(8,128)S(1)}, f32[2,2,64,3,128]{4,2,1,3,0:T(8,128)S(1)}, u32[]{:S(2)}, u32[]{:S(2)}) %collective-permute-start.1) | collective-permute-done | bytes 393248 | tf_op jit(solution)/shard_map/ppermute | solution.py:28
  47.8 1.0 collective-permute-done
  48.7 0.4 pad_maximum_fusion.1
  49.1 1.9 subtract_add_fusion.2
  51.0 2.2 multiply_add_fusion.2
  53.2 0.1 pad_maximum_fusion.7
  53.3 1.3 collective-permute-start.3
  54.6 17.5 %collective-permute-start.2 = (f32[2,2,64,3,128]{4,2,1,3,0:T(8,128)S(1)}, f32[2,2,64,3,128]{4,2,1,3,0:T(8,128)S(1)}, u32[]{:S(2)}, u32[]{:S(2)}) collective-permute-start(f32[2,2,64,3,128]{4,2,1,3,0:T(8,128)S(1)} %get-tuple-element.21), channel_id=1, source_target_pairs={{0,1},{1,2},{2,3},{3,4},{4,5},{5,6},{6,7},{7,8},{8,9},{9,10},{10,1... | collective-permute-start | bytes 1179656 | tf_op jit(solution)/shard_map/ppermute | solution.py:26
  72.1 1.2 fusion.26
  73.3 1.2 fusion.24
  74.5 3.7 collective-permute-done.3
  78.2 0.9 collective-permute-done.2
  79.1 0.4 pad_maximum_fusion.2
  79.5 1.8 subtract_add_fusion.1
  81.3 2.0 multiply_add_fusion.1
  83.3 0.1 pad_maximum_fusion.5
  83.4 1.3 collective-permute-start.5
  84.7 10.6 %collective-permute-start.4 = (f32[2,2,64,3,128]{4,2,1,3,0:T(8,128)S(1)}, f32[2,2,64,3,128]{4,2,1,3,0:T(8,128)S(1)}, u32[]{:S(2)}, u32[]{:S(2)}) collective-permute-start(f32[2,2,64,3,128]{4,2,1,3,0:T(8,128)S(1)} %get-tuple-element.17), channel_id=1, source_target_pairs={{0,1},{1,2},{2,3},{3,4},{4,5},{5,6},{6,7},{7,8},{8,9},{9,10},{10,1... | collective-permute-start | bytes 1179656 | tf_op jit(solution)/shard_map/ppermute | solution.py:26
  95.3 1.2 fusion.22
  96.5 1.2 fusion.20
  97.8 2.8 collective-permute-done.5
  100.6 1.0 collective-permute-done.4
  101.5 0.3 pad_maximum_fusion.3
  101.8 1.9 subtract_add_fusion
  103.7 2.1 multiply_subtract_fusion
  105.8 2.2 fusion.36
  108.0 2.2 fusion.40
  110.2 0.6 convolution_bitcast_fusion
  110.8 0.6 convolution_bitcast_fusion.2
  111.4 2.5 fusion
  113.8 2.3 fusion.1
  116.2 0.6 fusion.13
  116.8 0.1 copy.64
  116.8 0.6 fusion.11
  117.4 0.1 copy.63
  117.5 0.5 fusion.89
  118.1 0.5 fusion.91
  118.6 0.5 fusion.9
  119.2 0.5 fusion.8
  119.7 0.8 pad_maximum_fusion.4
  120.5 0.0 all-reduce.2.cloned.1.call-update
  120.6 0.0 reduce-scatter.2.cloned.1.call-start
  120.6 0.5 pad_maximum_fusion
  121.2 1.5 copy.60
  122.7 0.0 reduce-scatter.2.cloned.1.call-update
  122.7 312.2 %all-reduce.2.cloned.1.call-done = f32[2,8,64,64]{3,1,2,0:T(8,128)} async-done(((f32[2,8,64,64]{3,1,2,0:T(8,128)}), f32[2,8,64,64]{3,1,2,0:T(8,128)}) %all-reduce.2.cloned.1.call-update) | async-done | bytes 262160 | tf_op jit(solution)/shard_map/psum | solution.py:135
  434.9 1.9 copy.67
  (16 shorter events, 0.2 us)
Async XLA Ops:
  8.0 426.9 %all-reduce.2.cloned.1.call-start = ((), (), s32[]{:S(2)}) async-start(), calls=%async_computation.2 | async-start | bytes 1048576 | tf_op jit(solution)/shard_map/psum | solution.py:135
  8.1 20.3 %copy-start.1 = (f32[2,64,8,128]{3,2,1,0:T(8,128)S(1)}, f32[2,64,8,128]{3,2,1,0:T(8,128)}, u32[]{:S(2)}) copy-start(f32[2,64,8,128]{3,2,1,0:T(8,128)} %param.4) | copy-start | bytes 1572868
  8.1 20.3 %copy-start.3 = (f32[8,128]{1,0:T(8,128)S(1)}, f32[8,128]{1,0:T(8,128)}, u32[]{:S(2)}) copy-start(f32[8,128]{1,0:T(8,128)} %param.5) | copy-start | bytes 12292
  28.7 12.0 %copy-start = (f32[2,8,128,128]{3,2,1,0:T(8,128)S(1)}, f32[2,8,128,128]{3,2,1,0:T(8,128)}, u32[]{:S(2)}) copy-start(f32[2,8,128,128]{3,2,1,0:T(8,128)} %param.6) | copy-start | bytes 3145732
  28.9 13.0 %copy-start.2 = (f32[2,6,8,128]{3,2,1,0:T(8,128)S(1)}, f32[2,6,8,128]{3,2,1,0:T(8,128)}, u32[]{:S(2)}) copy-start(f32[2,6,8,128]{3,2,1,0:T(8,128)} %param.7) | copy-start | bytes 147460
  28.9 18.8 %collective-permute-start.1 = (f32[2,2,64,3,128]{4,2,1,3,0:T(8,128)S(1)}, f32[2,2,64,3,128]{4,2,1,3,0:T(8,128)S(1)}, u32[]{:S(2)}, u32[]{:S(2)}) collective-permute-start(f32[2,2,64,3,128]{4,2,1,3,0:T(8,128)S(1)} %get-tuple-element.24), channel_id=1, source_target_pairs={{1,0},{2,1},{3,2},{4,3},{5,4},{6,5},{7,6},{8,7},{9,8},{10,9},{11,1... | collective-permute-start | bytes 1179656 | tf_op jit(solution)/shard_map/ppermute | solution.py:28
  30.4 18.3 %collective-permute-start = (f32[2,2,64,3,128]{4,2,1,3,0:T(8,128)S(1)}, f32[2,2,64,3,128]{4,2,1,3,0:T(8,128)S(1)}, u32[]{:S(2)}, u32[]{:S(2)}) collective-permute-start(f32[2,2,64,3,128]{4,2,1,3,0:T(8,128)S(1)} %get-tuple-element.25), channel_id=1, source_target_pairs={{0,1},{1,2},{2,3},{3,4},{4,5},{5,6},{6,7},{7,8},{8,9},{9,10},{10,1... | collective-permute-start | bytes 1179656 | tf_op jit(solution)/shard_map/ppermute | solution.py:26
  53.3 24.9 %collective-permute-start.3 = (f32[2,2,64,3,128]{4,2,1,3,0:T(8,128)S(1)}, f32[2,2,64,3,128]{4,2,1,3,0:T(8,128)S(1)}, u32[]{:S(2)}, u32[]{:S(2)}) collective-permute-start(f32[2,2,64,3,128]{4,2,1,3,0:T(8,128)S(1)} %get-tuple-element.20), channel_id=1, source_target_pairs={{1,0},{2,1},{3,2},{4,3},{5,4},{6,5},{7,6},{8,7},{9,8},{10,9},{11,1... | collective-permute-start | bytes 1179656 | tf_op jit(solution)/shard_map/ppermute | solution.py:28
  54.6 24.5 %collective-permute-start.2 = (f32[2,2,64,3,128]{4,2,1,3,0:T(8,128)S(1)}, f32[2,2,64,3,128]{4,2,1,3,0:T(8,128)S(1)}, u32[]{:S(2)}, u32[]{:S(2)}) collective-permute-start(f32[2,2,64,3,128]{4,2,1,3,0:T(8,128)S(1)} %get-tuple-element.21), channel_id=1, source_target_pairs={{0,1},{1,2},{2,3},{3,4},{4,5},{5,6},{6,7},{7,8},{8,9},{9,10},{10,1... | collective-permute-start | bytes 1179656 | tf_op jit(solution)/shard_map/ppermute | solution.py:26
  83.4 17.2 %collective-permute-start.5 = (f32[2,2,64,3,128]{4,2,1,3,0:T(8,128)S(1)}, f32[2,2,64,3,128]{4,2,1,3,0:T(8,128)S(1)}, u32[]{:S(2)}, u32[]{:S(2)}) collective-permute-start(f32[2,2,64,3,128]{4,2,1,3,0:T(8,128)S(1)} %get-tuple-element.16), channel_id=1, source_target_pairs={{1,0},{2,1},{3,2},{4,3},{5,4},{6,5},{7,6},{8,7},{9,8},{10,9},{11,1... | collective-permute-start | bytes 1179656 | tf_op jit(solution)/shard_map/ppermute | solution.py:28
  84.7 16.8 %collective-permute-start.4 = (f32[2,2,64,3,128]{4,2,1,3,0:T(8,128)S(1)}, f32[2,2,64,3,128]{4,2,1,3,0:T(8,128)S(1)}, u32[]{:S(2)}, u32[]{:S(2)}) collective-permute-start(f32[2,2,64,3,128]{4,2,1,3,0:T(8,128)S(1)} %get-tuple-element.17), channel_id=1, source_target_pairs={{0,1},{1,2},{2,3},{3,4},{4,5},{5,6},{6,7},{7,8},{8,9},{9,10},{10,1... | collective-permute-start | bytes 1179656 | tf_op jit(solution)/shard_map/ppermute | solution.py:26
  120.6 316.2 %reduce-scatter.2.cloned.1.call-start = ((), (), s32[]{:S(2)}) async-start(), calls=%async_computation.1 | async-start | bytes 2359296 | tf_op jit(solution)/shard_map/reduce_scatter | solution.py:125
Sparse Core Ops, SparseCore 0:
  120.7 314.1 all-reduce.1
Sparse Core Ops, SparseCore 1:
  124.2 100.4 reduce-scatter.1
where the time goes:
time: 446 us; the launch traced here: 444 us
  waiting for transfers between devices  326 us (73%)
  starting transfers between devices  42.5 us (10%)
  matrix products  32.9 us (7%)
  local copies, waits for them, and re-layouts  24 us (5%)
  between operations  15.9 us (4%)
    psum x1, waiting for transfers between devices, on_device(): lax.psum(project(gram_re, gram_im, angles, scale), ('quad', 'dom'))  312 us
    ppermute x3, starting transfers between devices, with_halo(): lax.ppermute(tail, axis, [(i, (i + 1) % count) for i in range(ends)])  38.4 us
    unnamed x10, local copies, waits for them, and re-layouts  15.2 us
    ppermute x3, waiting for transfers between devices, with_halo(): lax.ppermute(head, axis, [((i + 1) % count, i) for i in range(ends)])  11 us
  transfers between devices with their start and end apart: 8, of which 7 were waited for; matrix products, arithmetic and copies ran while one was open for 3% of the time, Pallas kernels for 0%

commit v1 on v0

v1 whole, which is shorter than its diff:
```python
import functools
import math

import jax
import jax.numpy as jnp
import numpy as np
from jax import lax
from jax.experimental import pallas as pl
from jax.experimental.pallas import tpu as pltpu
from jax.sharding import PartitionSpec as P

NQ = 16
MOM = 4
RADIUS = 2.0
OFFSETS = (-3, -2, -1, 1, 2, 3)
LINES = 8
OWNED = 8
NY = 128
FIRST = 9
SPAN = 26
ORDER = (7, 0, 6, 1, 5, 4, 2, 3)
RIM = 6
NT = (((1,), (1,)), ((), ()))


def weights():
    theta = 2.0 * math.pi * (np.arange(NQ) + 0.5) / NQ
    return [[(RADIUS / NQ * math.cos(k * theta[a]), RADIUS / NQ * math.sin(k * theta[a])) for a in range(4)] for k in range(1, 2 * MOM + 1)]


WEIGHTS = weights()


def split(value):
    high = value.astype(jnp.bfloat16)
    low = (value - high.astype(jnp.float32)).astype(jnp.bfloat16)
    return high, low


def dot3(lhs_high, lhs_low, rhs_high, rhs_low):
    dot = functools.partial(lax.dot_general, dimension_numbers=NT, preferred_element_type=jnp.float32)
    return dot(lhs_high, rhs_high) + dot(lhs_low, rhs_high) + dot(lhs_high, rhs_low)


def sweep_kernel(
    doms, probes, mass, blocks, coup, table, mom_ref, proj_ref,
    zb, yb, zk, yk, pz, py, pe_own, pe_in, pack, inv_re, inv_im, src, cw, rhi, rlo,
    y1r, y1i, y2r, y2i, y3r, y3i, gram,
    zs_send, zs_recv, ys_send, ys_recv, sz_send, sz_recv, sy_send, sy_recv, ps_send, ps_recv, es_send, es_recv,
):
    q = lax.axis_index("quad")
    d = lax.axis_index("dom")
    c = lax.rem(q, 2)
    o = 1 - c
    zl = lax.div(q, 2)
    zh = lax.rem(d, 2)
    flip = d + 1 - 2 * zh
    up = lax.rem(d + 2, doms)
    down = lax.rem(d + doms - 2, doms)
    y_to = lax.rem(d + 2 - 4 * zh + doms, doms)
    at_top = lax.div(q + 2, 8)
    at_bottom = 1 - lax.div(q + 6, 8)
    head = (1 - c) * at_top + c * at_bottom
    tail = (1 - c) * at_bottom + c * at_top
    q_to = lax.rem(q + 8 + 2 - 4 * c, 8)
    q_from = lax.rem(q + 8 - 2 + 4 * c, 8)
    d_to = d + head * (1 - 2 * zh)
    d_from = d + tail * (1 - 2 * zh)
    sib = q + 1 - 2 * c
    mirror = 2 * (3 - zl) + c
    is_head = head == 1

    barrier = pltpu.get_barrier_semaphore()

    def greet(quad, dom):
        pl.semaphore_signal(barrier, inc=1, device_id={"quad": quad, "dom": dom}, device_id_type=pl.DeviceIdType.MESH)

    greet(q_from, d_from)
    greet(sib, d)
    greet(mirror, flip)
    greet(q, up)
    greet(q, down)

    def copy(source, target, send, recv, quad, dom):
        return pltpu.make_async_remote_copy(
            src_ref=source, dst_ref=target, send_sem=send, recv_sem=recv,
            device_id={"quad": quad, "dom": dom}, device_id_type=pl.DeviceIdType.MESH,
        )

    def z_copy(s):
        if s == 0:
            return copy(zk.at[c], zk.at[c], zs_send.at[0], zs_recv.at[0], q_to, d_to)
        t = ORDER[s - 1]
        return copy(zb.at[c, t], zb.at[c, t], zs_send.at[s], zs_recv.at[s], q_to, d_to)

    def z_head(s):
        if s == 0:
            return copy(pack.at[c], zk.at[c], zs_send.at[0], zs_recv.at[0], q_to, d_to)
        t = ORDER[s - 1]
        line = zh * t + (1 - zh) * (LINES - 1 - t)
        return copy(blocks.at[c, line], zb.at[c, t], zs_send.at[s], zs_recv.at[s], q_to, d_to)

    def y_pack():
        return copy(zk.at[c], yk.at[c], ys_send.at[RIM], ys_recv.at[RIM], q, y_to)

    def y_copy(u):
        return copy(zb.at[c, LINES - 1 - u], yb.at[c, u], ys_send.at[u], ys_recv.at[u], q, y_to)

    def sz_pack(part):
        return copy(zk.at[part], zk.at[part], sz_send.at[RIM], sz_recv.at[RIM], sib, d)

    def sz_copy(t, part):
        return copy(zb.at[part, t], zb.at[part, t], sz_send.at[t], sz_recv.at[t], sib, d)

    def sy_pack(part):
        return copy(yk.at[part], yk.at[part], sy_send.at[RIM], sy_recv.at[RIM], sib, d)

    def sy_copy(u, part):
        return copy(yb.at[part, u], yb.at[part, u], sy_send.at[u], sy_recv.at[u], sib, d)

    p_mirror = copy(probes.at[:, pl.ds(mirror * OWNED * LINES, OWNED * LINES), :], pz, ps_send.at[0], ps_recv.at[0], mirror, flip)
    p_next = copy(pz, py, ps_send.at[1], ps_recv.at[1], q, y_to)
    e_up = copy(pe_own.at[1], pe_in.at[1], es_send.at[1], es_recv.at[1], q, up)
    e_down = copy(pe_own.at[0], pe_in.at[0], es_send.at[0], es_recv.at[0], q, down)

    eye = lax.broadcasted_iota(jnp.int32, (NY, NY), 0) == lax.broadcasted_iota(jnp.int32, (NY, NY), 1)

    for part in range(2):
        pack[part, 0:48, :] = coup[part]
        pack[part, 56:64, :] = mass[...]

    @pl.loop(0, LINES)
    def _(line):
        for part in range(2):
            diagonal = jnp.sum(jnp.where(eye, blocks[part, line], 0.0), axis=0, keepdims=True)
            pack[part, pl.ds(48 + line, 1), :] = diagonal

    for side, line in ((0, 0), (1, LINES - 1)):
        for part in range(2):
            pe_own[side, 8 * part : 8 * part + 8, :] = probes[part, pl.ds(q * OWNED * LINES + line, OWNED, stride=LINES), :]
            pe_own[side, 17 + part : 18 + part, :] = pack[part, 48 + line : 49 + line, :]
        pe_own[side, 16:17, :] = mass[line : line + 1, :]

    pl.semaphore_wait(barrier, 5)

    p_mirror.start()

    @pl.when(is_head)
    def _():
        for s in range(len(ORDER) + 1):
            z_head(s).start()

    e_up.start()
    e_down.start()

    def prepare(w, probe_re, probe_im, weight, diag_re, diag_im):
        line = d * LINES + zh * (w - FIRST) + (1 - zh) * (SPAN - 1 - FIRST - w)
        inside = jnp.logical_and(line >= 0, line < doms * LINES)
        source_re = weight * probe_re
        source_im = weight * probe_im
        src[w, 0] = source_re
        src[w, 1] = source_im
        denom_re = table[0] * weight - diag_re
        denom_im = table[1] * weight - diag_im
        modulus = denom_re * denom_re + denom_im * denom_im
        inv_re[w] = jnp.where(inside, denom_re / modulus, 0.0)
        inv_im[w] = jnp.where(inside, -denom_im / modulus, 0.0)
        for j in range(NQ):
            g_re = inv_re[w, j : j + 1, :]
            g_im = inv_im[w, j : j + 1, :]
            y1r[w, 8 * j : 8 * j + 8, :] = source_re * g_re - source_im * g_im
            y1i[w, 8 * j : 8 * j + 8, :] = source_re * g_im + source_im * g_re

    def couple(w, ref, line):
        for position in range(6):
            row = zh * position + (1 - zh) * (5 - position)
            for part in range(2):
                cw[w, 6 * part + position : 6 * part + position + 1, :] = ref[part, pl.ds(row * LINES + line, 1), :]

    def prepare_packed(w, line, probe, packed):
        couple(w, packed, line)
        prepare(
            w,
            probe[0, pl.ds(line, OWNED, stride=LINES), :],
            probe[1, pl.ds(line, OWNED, stride=LINES), :],
            packed[0, pl.ds(56 + line, 1), :],
            packed[0, pl.ds(48 + line, 1), :],
            packed[1, pl.ds(48 + line, 1), :],
        )

    def prepare_edge(w, side):
        prepare(w, pe_in[side, 0:8, :], pe_in[side, 8:16, :], pe_in[side, 16:17, :], pe_in[side, 17:18, :], pe_in[side, 18:19, :])

    def own_line(w):
        return zh * (w - FIRST) + (1 - zh) * (SPAN - 1 - FIRST - w)

    def operand(w, block_re, block_im):
        re_high, re_low = split(jnp.where(eye, 0.0, block_re))
        im_high, im_low = split(jnp.where(eye, 0.0, block_im))
        for ref, re, im in ((rhi, re_high, im_high), (rlo, re_low, im_low)):
            ref[w - 3, 0:NY, 0:NY] = re
            ref[w - 3, 0:NY, NY:] = -im
            ref[w - 3, NY:, 0:NY] = im
            ref[w - 3, NY:, NY:] = re

    def sweep(yr, yi, w, emit, order=range(NQ)):
        high, low = split(jnp.concatenate([yr[w], yi[w]], axis=1))
        image = dot3(high, low, rhi[w - 3], rlo[w - 3])
        c_re = [cw[w, i : i + 1, :] for i in range(6)]
        c_im = [cw[w, 6 + i : 7 + i, :] for i in range(6)]
        source_re = src[w, 0]
        source_im = src[w, 1]
        for j in order:
            rows = slice(8 * j, 8 * j + 8)
            a_re = image[rows, :NY] + source_re
            a_im = image[rows, NY:] + source_im
            for i, offset in enumerate(OFFSETS):
                n_re = yr[w + offset, rows, :]
                n_im = yi[w + offset, rows, :]
                a_re = a_re + (c_re[i] * n_re - c_im[i] * n_im)
                a_im = a_im + (c_re[i] * n_im + c_im[i] * n_re)
            g_re = inv_re[w, j : j + 1, :]
            g_im = inv_im[w, j : j + 1, :]
            emit(j, g_re * a_re - g_im * a_im, g_re * a_im + g_im * a_re)

    def second(w):
        def emit(j, re, im):
            y2r[w, 8 * j : 8 * j + 8, :] = re
            y2i[w, 8 * j : 8 * j + 8, :] = im

        sweep(y1r, y1i, w, emit)

    def third(w):
        def emit(j, re, im):
            y3r[w, 8 * j : 8 * j + 8, :] = re
            y3i[w, 8 * j : 8 * j + 8, :] = im

        sweep(y2r, y2i, w, emit)

    def last(w):
        line = own_line(w)
        field = {}

        def emit(j, re, im):
            field[j] = (re, im)

        sweep(y3r, y3i, w, emit, [a + 4 * b for a in range(4) for b in range(4)])
        sum_re = [None] * (2 * MOM)
        sum_im = [None] * (2 * MOM)
        for a in range(4):
            (r0, i0), (r1, i1), (r2, i2), (r3, i3) = (field[a + 4 * b] for b in range(4))
            er, ei, fr, fi = r0 + r2, i0 + i2, r0 - r2, i0 - i2
            gr, gi, hr, hi = r1 + r3, i1 + i3, r1 - r3, i1 - i3
            groups = ((er + gr, ei + gi), (fr - hi, fi + hr), (er - gr, ei - gi), (fr + hi, fi - hr))
            for k in range(2 * MOM):
                x_re, x_im = groups[(k + 1) % 4]
                w_re, w_im = WEIGHTS[k][a]
                t_re = w_re * x_re - w_im * x_im
                t_im = w_re * x_im + w_im * x_re
                sum_re[k] = t_re if a == 0 else sum_re[k] + t_re
                sum_im[k] = t_im if a == 0 else sum_im[k] + t_im
        for k in range(MOM):
            mom_ref[pl.ds(k * 16 + line, OWNED, stride=64), :] = sum_re[k]
            mom_ref[pl.ds(k * 16 + 8 + line, OWNED, stride=64), :] = sum_im[k]
        m_high, m_low = split(jnp.concatenate(sum_re + sum_im, axis=0))
        v_high, v_low = split(jnp.concatenate([probes[part, pl.ds(line, 64, stride=LINES), :] for part in range(2)], axis=0))
        gram[...] += dot3(v_high, v_low, m_high, m_low)

    def relay(s):
        z_copy(s).wait_recv()
        if s == 0:
            y_pack().start()
        elif ORDER[s - 1] >= 2:
            y_copy(LINES - 1 - ORDER[s - 1]).start()

        @pl.when(head == 0)
        def _():
            z_copy(s).start()

        if s == 0:
            sz_pack(c).start()
        elif ORDER[s - 1] < RIM:
            sz_copy(ORDER[s - 1], c).start()

    gram[...] = jnp.zeros_like(gram)

    @pl.loop(FIRST, FIRST + LINES)
    def _(w):
        line = own_line(w)
        couple(w, coup, line)
        prepare(
            w,
            probes[0, pl.ds(q * OWNED * LINES + line, OWNED, stride=LINES), :],
            probes[1, pl.ds(q * OWNED * LINES + line, OWNED, stride=LINES), :],
            mass[pl.ds(line, 1), :],
            pack[0, pl.ds(48 + line, 1), :],
            pack[1, pl.ds(48 + line, 1), :],
        )

    p_mirror.wait_recv()
    p_next.start()
    relay(0)
    relay(1)
    relay(2)

    @pl.loop(FIRST, FIRST + LINES)
    def _(w):
        line = own_line(w)
        operand(w, blocks[0, line], blocks[1, line])

    relay(3)
    sz_pack(o).wait_recv()
    e_down.wait_recv()
    e_up.wait_recv()

    @pl.loop(0, LINES)
    def _(t):
        prepare_packed(FIRST - 1 - t, (1 - zh) * t + zh * (LINES - 1 - t), pz, zk)

    prepare_edge(0, zh)
    relay(4)
    pl.loop(FIRST, FIRST + 2)(second)
    relay(5)
    pl.loop(FIRST + 2, FIRST + 4)(second)
    relay(6)
    pl.loop(FIRST + 4, FIRST + 5)(second)
    relay(7)
    relay(8)
    y_pack().wait_recv()
    sy_pack(c).start()
    for t in range(RIM):
        sz_copy(t, o).wait_recv()

    @pl.loop(0, RIM)
    def _(t):
        w = FIRST - 1 - t
        operand(w, zb[0, t], zb[1, t])
        second(w)

    p_next.wait_recv()
    sy_pack(o).wait_recv()

    @pl.loop(0, LINES)
    def _(u):
        prepare_packed(FIRST + LINES + u, (1 - zh) * (LINES - 1 - u) + zh * u, py, yk)

    prepare_edge(SPAN - 1, 1 - zh)
    y_copy(0).wait_recv()
    sy_copy(0, c).start()
    pl.loop(FIRST + 5, FIRST + 8)(second)
    pl.loop(FIRST - 3, FIRST + 5)(third)
    pl.loop(FIRST, FIRST + 2)(last)

    @pl.loop(0, RIM)
    def _(u):
        @pl.when(u < RIM - 1)
        def _():
            y_copy(u + 1).wait_recv()
            sy_copy(u + 1, c).start()

        sy_copy(u, o).wait_recv()
        w = FIRST + LINES + u
        operand(w, yb[0, u], yb[1, u])
        second(w)
        third(w - 3)
        last(w - 6)

    lane = lax.broadcasted_iota(jnp.int32, (64, 128), 1)
    other = pltpu.roll(gram[64:, :], 64, 1)
    scale = 1.0 / float(doms * LINES * NY)
    proj_ref[...] = scale * (gram[:64, :] + jnp.where(lane < 64, other, -other))

    p_mirror.wait_send()
    p_next.wait_send()
    e_up.wait_send()
    e_down.wait_send()
    for s in range(len(ORDER) + 1):
        z_copy(s).wait_send()
    y_pack().wait_send()
    sz_pack(c).wait_send()
    sy_pack(c).wait_send()
    for i in range(RIM):
        y_copy(i).wait_send()
        sz_copy(i, c).wait_send()
        sy_copy(i, c).wait_send()


def reduce_kernel(planes, part_ref, out_ref, mine, gathered, column, total, full, s1, r1, s2, r2, s3, r3):
    q = lax.axis_index("quad")
    d = lax.axis_index("dom")
    zh = lax.rem(d, 2)
    m = lax.div(d, 2)
    slot = zh * 8 + q
    rows = 64 // planes

    def dev(quad, dom):
        return {"quad": quad, "dom": dom}

    barrier = pltpu.get_barrier_semaphore()

    @pl.loop(1, planes)
    def _(i):
        pl.semaphore_signal(barrier, inc=1, device_id=dev(q, lax.rem(m + i, planes) * 2 + zh), device_id_type=pl.DeviceIdType.MESH)

    @pl.loop(1, 16)
    def _(i):
        to = lax.rem(slot + i, 16)
        pl.semaphore_signal(barrier, inc=1, device_id=dev(lax.rem(to, 8), 2 * m + lax.div(to, 8)), device_id_type=pl.DeviceIdType.MESH)

    for i in range(planes):
        mine[i] = part_ref[i * rows : (i + 1) * rows, :]
    pl.semaphore_wait(barrier, planes - 1 + 15)

    def plane_copy(i):
        to = lax.rem(m + i, planes)
        return pltpu.make_async_remote_copy(
            src_ref=mine.at[to], dst_ref=gathered.at[i], send_sem=s1.at[i], recv_sem=r1.at[i],
            device_id=dev(q, to * 2 + zh), device_id_type=pl.DeviceIdType.MESH,
        )

    def column_copy(i):
        to = lax.rem(slot + i, 16)
        return pltpu.make_async_remote_copy(
            src_ref=column.at[slot], dst_ref=column.at[slot], send_sem=s2.at[i], recv_sem=r2.at[i],
            device_id=dev(lax.rem(to, 8), 2 * m + lax.div(to, 8)), device_id_type=pl.DeviceIdType.MESH,
        )

    def column_arrived(i):
        come = lax.rem(slot + 16 - i, 16)
        return pltpu.make_async_remote_copy(
            src_ref=column.at[come], dst_ref=column.at[come], send_sem=s2.at[i], recv_sem=r2.at[i],
            device_id=dev(lax.rem(come, 8), 2 * m + lax.div(come, 8)), device_id_type=pl.DeviceIdType.MESH,
        )

    def full_copy(i):
        to = lax.rem(m + i, planes)
        return pltpu.make_async_remote_copy(
            src_ref=total, dst_ref=full.at[m], send_sem=s3.at[i], recv_sem=r3.at[i],
            device_id=dev(q, to * 2 + zh), device_id_type=pl.DeviceIdType.MESH,
        )

    def full_arrived(i):
        come = lax.rem(m + planes - i, planes)
        return pltpu.make_async_remote_copy(
            src_ref=total, dst_ref=full.at[come], send_sem=s3.at[i], recv_sem=r3.at[i],
            device_id=dev(q, come * 2 + zh), device_id_type=pl.DeviceIdType.MESH,
        )

    @pl.loop(1, planes)
    def _(i):
        plane_copy(i).start()

    gathered[0] = mine[m]

    @pl.loop(1, planes)
    def _(i):
        plane_copy(i).wait_recv()

    column[slot] = functools.reduce(lambda a, b: a + b, [gathered[i] for i in range(planes)])

    @pl.loop(1, 16)
    def _(i):
        column_copy(i).start()

    @pl.loop(1, 16)
    def _(i):
        column_arrived(i).wait_recv()

    for i in range(8):
        total[i] = column[i] + column[8 + i]

    @pl.loop(1, planes)
    def _(i):
        full_copy(i).start()

    full[m] = total[...]

    @pl.loop(1, planes)
    def _(i):
        full_arrived(i).wait_recv()

    out_ref[...] = full[...]

    @pl.loop(1, planes)
    def _(i):
        plane_copy(i).wait_send()
        full_copy(i).wait_send()

    @pl.loop(1, 16)
    def _(i):
        column_copy(i).wait_send()


def on_device(doms, probes, mass_weights, blocks, couplings):
    f32 = jnp.float32
    theta = 2.0 * math.pi * (np.arange(NQ) + 0.5) / NQ
    table = jnp.asarray(np.broadcast_to(np.stack([RADIUS * np.cos(theta), RADIUS * np.sin(theta)])[:, :, None], (2, NQ, NY)), f32)
    vmem = pl.BlockSpec(memory_space=pltpu.VMEM)
    dma = pltpu.SemaphoreType.DMA
    moments, partial = pl.pallas_call(
        functools.partial(sweep_kernel, doms),
        out_shape=(jax.ShapeDtypeStruct((512, NY), f32), jax.ShapeDtypeStruct((64, NY), f32)),
        in_specs=[vmem] * 5,
        out_specs=(vmem, vmem),
        scratch_shapes=[
            pltpu.VMEM((2, LINES, NY, NY), f32),
            pltpu.VMEM((2, RIM, NY, NY), f32),
            pltpu.VMEM((2, 64, NY), f32),
            pltpu.VMEM((2, 64, NY), f32),
            pltpu.VMEM((2, 64, NY), f32),
            pltpu.VMEM((2, 64, NY), f32),
            pltpu.VMEM((2, 24, NY), f32),
            pltpu.VMEM((2, 24, NY), f32),
            pltpu.VMEM((2, 64, NY), f32),
            pltpu.VMEM((SPAN, NQ, NY), f32),
            pltpu.VMEM((SPAN, NQ, NY), f32),
            pltpu.VMEM((SPAN, 2, OWNED, NY), f32),
            pltpu.VMEM((SPAN, 16, NY), f32),
            pltpu.VMEM((20, 2 * NY, 2 * NY), jnp.bfloat16),
            pltpu.VMEM((20, 2 * NY, 2 * NY), jnp.bfloat16),
        ]
        + [pltpu.VMEM((SPAN, NQ * OWNED, NY), f32)] * 6
        + [pltpu.VMEM((NY, NY), f32)]
        + [dma((9,)), dma((9,)), dma((7,)), dma((7,)), dma((7,)), dma((7,)), dma((7,)), dma((7,)), dma((2,)), dma((2,)), dma((2,)), dma((2,))],
        compiler_params=pltpu.CompilerParams(collective_id=0, has_side_effects=True, vmem_limit_bytes=48 * 1024 * 1024),
    )(
        probes.reshape(2, 512, NY),
        mass_weights,
        blocks,
        couplings.reshape(2, 48, NY),
        table,
    )
    planes = doms // 2
    rows = 64 // planes
    full = pl.pallas_call(
        functools.partial(reduce_kernel, planes),
        out_shape=jax.ShapeDtypeStruct((planes, 8, rows, NY), f32),
        in_specs=[vmem],
        out_specs=vmem,
        scratch_shapes=[
            pltpu.VMEM((planes, rows, NY), f32),
            pltpu.VMEM((planes, rows, NY), f32),
            pltpu.VMEM((16, rows, NY), f32),
            pltpu.VMEM((8, rows, NY), f32),
            pltpu.VMEM((planes, 8, rows, NY), f32),
        ]
        + [dma((16,))] * 6,
        compiler_params=pltpu.CompilerParams(collective_id=1, has_side_effects=True),
    )(partial)
    projected = full.reshape(planes, 8, rows, 2, 8, 8).transpose(3, 4, 0, 2, 1, 5).reshape(2, 8, 64, 64)
    return moments.reshape(OWNED, MOM, 2, LINES, NY), projected


def solution(mesh):
    return jax.shard_map(
        functools.partial(on_device, mesh.shape["dom"]),
        mesh=mesh,
        in_specs=(P(None, None, "dom", None), P("dom", None), P(None, "dom", None, None), P(None, None, "dom", None)),
        out_specs=(P("quad", None, None, "dom", None), P()),
        check_vma=False,
    )
```

time: 446 us -> 89.6 us (0.20)
  waiting for transfers between devices: 326 us -> 0 us
  Pallas kernels: 0 us -> 72.9 us
  starting transfers between devices: 42.5 us -> 0 us
  matrix products: 32.9 us -> 0 us
  between operations: 15.9 us -> 0.68 us
  local copies, waits for them, and re-layouts: 24 us -> 15.7 us
    psum x1 -> x0, waiting for transfers between devices: 312 us -> none  [on_device(): lax.psum(project(gram_re, gram_im, angles, scale), ('quad', 'dom'))]
    pallas_call x0 -> x2, Pallas kernels: none -> 72.9 us  [the longest x1 52.8 us: on_device(): pl.pallas_call(functools.partial(sweep_kernel, doms), out_shape=(jax.Shap...]
    ppermute x6 -> x0, starting transfers between devices: 42.4 us -> none  [the longest x3 38.4 us: with_halo(): lax.ppermute(tail, axis, [(i, (i + 1) % count) for i in range(ends)])]
    dot_general x24 -> x0, matrix products: 32.9 us -> none  [the longest x3 6.29 us: sweep(): jnp.einsum('spxj,xij->spxi', field_re, blocks[1], precision=PRECISE)]
    ppermute x6 -> x0, waiting for transfers between devices: 13.8 us -> none  [the longest x3 11 us: with_halo(): lax.ppermute(head, axis, [((i + 1) % count, i) for i in range(ends)])]
    unnamed x10 -> x13, local copies, waits for them, and re-layouts: 15.2 us -> 5.77 us
    gather x1 -> x0, local copies, waits for them, and re-layouts: 6.69 us -> none  [on_device(): diagonal = jnp.diagonal(blocks, axis1=2, axis2=3)]
  transfers between devices with their start and end apart: 8 -> 0, of which waited for: 7 -> 0; matrix products, arithmetic and copies ran while one was open for 3% -> 0% of each run, Pallas kernels for 0% -> 0%
where the time goes in v1:
time: 89.6 us; the launch traced here: 89.2 us
  Pallas kernels  72.9 us (81%)
  local copies, waits for them, and re-layouts  15.7 us (18%)
    pallas_call x1, Pallas kernels, on_device(): pl.pallas_call(functools.partial(sweep_kernel, doms), out_shape=(jax.Shap...  52.8 us
    pallas_call x1, Pallas kernels, on_device(): pl.pallas_call(functools.partial(reduce_kernel, planes), out_shape=jax.Sh...  20 us
    unnamed x13, local copies, waits for them, and re-layouts  5.77 us
    transpose x1, local copies, waits for them, and re-layouts, on_device(): full.reshape(planes, 8, rows, 2, 8, 8).transpose(3, 4, 0, 2, 1, 5)  4.38 us
    reshape x1, local copies, waits for them, and re-layouts, on_device(): full.reshape(planes, 8, rows, 2, 8, 8).transpose(3, 4, 0, 2, 1, 5)  3.94 us

profile of v1, /device:TPU:1, one launch (start us, length us, event | category | flops | bytes accessed | tf_op | source)
XLA Modules:
  0.0 89.2 jit_solution(3499448044662971727)
XLA Ops:
  0.6 0.0 copy-start
  0.6 1.2 %copy-done = f32[2,8,128,128]{3,2,1,0:T(8,128)S(1)} copy-done((f32[2,8,128,128]{3,2,1,0:T(8,128)S(1)}, f32[2,8,128,128]{3,2,1,0:T(8,128)}, u32[]{:S(2)}) %copy-start) | copy-done | bytes 1048600
  1.9 0.0 copy-start.1
  1.9 1.0 %copy-done.1 = f32[2,64,8,128]{3,2,1,0:T(8,128)S(1)} copy-done((f32[2,64,8,128]{3,2,1,0:T(8,128)S(1)}, f32[2,64,8,128]{3,2,1,0:T(8,128)}, u32[]{:S(2)}) %copy-start.1) | copy-done | bytes 524312
  2.9 0.0 copy-start.2
  2.9 0.8 copy-done.2
  3.7 0.0 copy-start.4
  3.7 0.7 copy-done.4
  4.4 0.0 copy-start.5
  4.4 0.7 copy-done.5
  5.1 52.8 %shard_map.68 = (f32[512,128]{1,0:T(8,128)S(1)}, f32[64,128]{1,0:T(8,128)S(1)}) custom-call(f32[2,512,128]{2,1,0:T(8,128)S(1)} %bitcast.8, f32[8,128]{1,0:T(8,128)S(1)} %copy-done.5, f32[2,8,128,128]{3,2,1,0:T(8,128)S(1)} %copy-done, f32[2,48,128]{2,1,0:T(8,128)S(1)} %bitcast.10, f32[2,16,128]{2,1,0:T(8,128)S(1)} %copy-done.4), custom_call_target="tpu_custom_call" | custom-call | tf_op jit(solution)/shard_map/pallas_call | solution.py:500
  57.9 0.0 copy-start.3
  57.9 0.6 copy-done.3
  58.5 20.0 %shard_map.69 = f32[16,8,4,128]{3,2,1,0:T(4,128)} custom-call(f32[64,128]{1,0:T(8,128)} %copy-done.3), custom_call_target="tpu_custom_call" | custom-call | tf_op jit(solution)/shard_map/pallas_call | solution.py:535
  78.6 1.6 %copy.8 = f32[16,8,4,128]{0,3,2,1:T(8,128)S(1)} copy(f32[16,8,4,128]{3,2,1,0:T(4,128)} %shard_map.69) | data formatting | bytes 524288 | tf_op jit(solution)/shard_map/pallas_call | solution.py:535
  80.2 4.4 %copy.9 = f32[2,8,16,4,8,8]{5,4,3,2,1,0:T(8,128)} copy(f32[2,8,16,4,8,8]{2,5,1,0,3,4:T(8,128)S(1)} %bitcast.11) | data formatting | bytes 524288 | tf_op jit(solution)/shard_map/transpose | solution.py:550
  84.5 3.9 %reshape.23 = f32[2,8,64,64]{3,2,1,0:T(8,128)} reshape(f32[2,8,16,4,8,8]{5,4,3,2,1,0:T(8,128)} %copy.9) | data formatting | bytes 524288 | tf_op jit(solution)/shard_map/reshape | solution.py:550
  88.5 0.7 copy.11
Async XLA Ops:
  0.6 1.2 %copy-start = (f32[2,8,128,128]{3,2,1,0:T(8,128)S(1)}, f32[2,8,128,128]{3,2,1,0:T(8,128)}, u32[]{:S(2)}) copy-start(f32[2,8,128,128]{3,2,1,0:T(8,128)} %blocks.1) | copy-start | bytes 3145732
  1.9 1.0 %copy-start.1 = (f32[2,64,8,128]{3,2,1,0:T(8,128)S(1)}, f32[2,64,8,128]{3,2,1,0:T(8,128)}, u32[]{:S(2)}) copy-start(f32[2,64,8,128]{3,2,1,0:T(8,128)} %param.5) | copy-start | bytes 1572868
  2.9 0.8 copy-start.2
  3.7 0.7 copy-start.4
  4.4 0.7 copy-start.5
  57.9 0.6 copy-start.3

commit v2 on v1

v2 whole, which is shorter than its diff:
```python
import functools
import math

import jax
import jax.numpy as jnp
import numpy as np
from jax import lax
from jax.experimental import pallas as pl
from jax.experimental.pallas import tpu as pltpu
from jax.sharding import PartitionSpec as P

NQ = 16
MOM = 4
RADIUS = 2.0
OFFSETS = (-3, -2, -1, 1, 2, 3)
LINES = 8
OWNED = 8
NY = 128
FIRST = 9
SPAN = 26
ORDER = (7, 0, 6, 1, 5, 4, 3, 2)
RIM = 6
NT = (((1,), (1,)), ((), ()))


def weights():
    theta = 2.0 * math.pi * (np.arange(NQ) + 0.5) / NQ
    return [[(RADIUS / NQ * math.cos(k * theta[a]), RADIUS / NQ * math.sin(k * theta[a])) for a in range(4)] for k in range(1, 2 * MOM + 1)]


WEIGHTS = weights()


def split(value):
    high = value.astype(jnp.bfloat16)
    low = (value - high.astype(jnp.float32)).astype(jnp.bfloat16)
    return high, low


def dot3(lhs, rhs_high, rhs_low):
    dot = functools.partial(lax.dot_general, dimension_numbers=NT, preferred_element_type=jnp.float32)
    high, low = split(lhs)
    count = lhs.shape[0]
    both = dot(jnp.concatenate([high, low], axis=0), rhs_high)
    return both[:count] + both[count:] + dot(high, rhs_low)


def sweep_kernel(
    doms, probes_hbm, mass_hbm, blocks_hbm, coup_hbm, mom_ref, out_ref,
    probes, blocks, table, zb, yb, zk, yk, pz, py, pe_own, pe_in, pack, inv_re, inv_im, src, cw, rhi, rlo,
    y1r, y1i, y2r, y2i, y3r, y3i, ima, imb, imc, gram, mine, gathered, column, total, full,
    in_sem, zs_send, zs_recv, ys_send, ys_recv, sz_send, sz_recv, sy_send, sy_recv, ps_send, ps_recv, es_send, es_recv,
    s1, r1, s2, r2, s3, r3,
):
    q = lax.axis_index("quad")
    d = lax.axis_index("dom")
    c = lax.rem(q, 2)
    o = 1 - c
    zl = lax.div(q, 2)
    zh = lax.rem(d, 2)
    flip = d + 1 - 2 * zh
    up = lax.rem(d + 2, doms)
    down = lax.rem(d + doms - 2, doms)
    y_to = lax.rem(d + 2 - 4 * zh + doms, doms)
    at_top = lax.div(q + 2, 8)
    at_bottom = 1 - lax.div(q + 6, 8)
    head = (1 - c) * at_top + c * at_bottom
    tail = (1 - c) * at_bottom + c * at_top
    q_to = lax.rem(q + 8 + 2 - 4 * c, 8)
    q_from = lax.rem(q + 8 - 2 + 4 * c, 8)
    d_to = d + head * (1 - 2 * zh)
    d_from = d + tail * (1 - 2 * zh)
    sib = q + 1 - 2 * c
    mirror = 2 * (3 - zl) + c
    is_head = head == 1
    far = lax.div(c * (3 - zl) + (1 - c) * zl, 2) == 1
    planes = doms // 2
    rows = 64 // planes
    m = lax.div(d, 2)
    slot = zh * 8 + q

    arrivals = [
        pltpu.make_async_copy(coup_hbm, pack.at[:, pl.ds(0, 48), :], in_sem.at[0]),
        pltpu.make_async_copy(mass_hbm, pack.at[0, pl.ds(56, 8), :], in_sem.at[1]),
        pltpu.make_async_copy(mass_hbm, pack.at[1, pl.ds(56, 8), :], in_sem.at[2]),
        pltpu.make_async_copy(probes_hbm, probes, in_sem.at[3]),
        pltpu.make_async_copy(blocks_hbm, blocks, in_sem.at[4]),
    ]
    for arrival in arrivals:
        arrival.start()

    barrier = pltpu.get_barrier_semaphore()

    def greet(quad, dom):
        pl.semaphore_signal(barrier, inc=1, device_id={"quad": quad, "dom": dom}, device_id_type=pl.DeviceIdType.MESH)

    greet(mirror, flip)
    greet(q_from, d_from)
    greet(q, up)
    greet(q, down)
    greet(sib, d)

    @pl.loop(1, planes)
    def _(i):
        greet(q, lax.rem(m + i, planes) * 2 + zh)

    @pl.loop(1, 16)
    def _(i):
        to = lax.rem(slot + i, 16)
        greet(lax.rem(to, 8), 2 * m + lax.div(to, 8))

    def copy(source, target, send, recv, quad, dom):
        return pltpu.make_async_remote_copy(
            src_ref=source, dst_ref=target, send_sem=send, recv_sem=recv,
            device_id={"quad": quad, "dom": dom}, device_id_type=pl.DeviceIdType.MESH,
        )

    def z_copy(s):
        t = ORDER[s]
        return copy(zb.at[c, t], zb.at[c, t], zs_send.at[s], zs_recv.at[s], q_to, d_to)

    def z_head(s):
        t = ORDER[s]
        line = zh * t + (1 - zh) * (LINES - 1 - t)
        return copy(blocks_hbm.at[c, line], zb.at[c, t], zs_send.at[s], zs_recv.at[s], q_to, d_to)

    def y_pack():
        return copy(zk.at[c], yk.at[c], ys_send.at[RIM], ys_recv.at[RIM], q, y_to)

    def y_copy(u):
        return copy(zb.at[c, LINES - 1 - u], yb.at[c, u], ys_send.at[u], ys_recv.at[u], q, y_to)

    def sz_pack(part):
        return copy(zk.at[part], zk.at[part], sz_send.at[RIM], sz_recv.at[RIM], sib, d)

    def sz_copy(t, part):
        return copy(zb.at[part, t], zb.at[part, t], sz_send.at[t], sz_recv.at[t], sib, d)

    def sy_pack(part):
        return copy(yk.at[part], yk.at[part], sy_send.at[RIM], sy_recv.at[RIM], sib, d)

    def sy_copy(u, part):
        return copy(yb.at[part, u], yb.at[part, u], sy_send.at[u], sy_recv.at[u], sib, d)

    k_mirror = copy(pack.at[c], zk.at[c], ps_send.at[2], ps_recv.at[2], mirror, flip)
    p_mirror = copy(probes_hbm.at[:, pl.ds(mirror * OWNED * LINES, OWNED * LINES), :], pz, ps_send.at[0], ps_recv.at[0], mirror, flip)
    p_next = copy(pz, py, ps_send.at[1], ps_recv.at[1], q, y_to)
    e_up = copy(pe_own.at[1], pe_in.at[1], es_send.at[1], es_recv.at[1], q, up)
    e_down = copy(pe_own.at[0], pe_in.at[0], es_send.at[0], es_recv.at[0], q, down)

    eye = lax.broadcasted_iota(jnp.int32, (NY, NY), 0) == lax.broadcasted_iota(jnp.int32, (NY, NY), 1)

    row = lax.broadcasted_iota(jnp.int32, (NQ, NY), 0)
    for part, function in ((0, math.cos), (1, math.sin)):
        values = jnp.zeros((NQ, NY), jnp.float32)
        for j in range(NQ):
            values = jnp.where(row == j, RADIUS * function(2.0 * math.pi * (j + 0.5) / NQ), values)
        table[part] = values
    for arrival in arrivals:
        arrival.wait()

    @pl.loop(0, LINES)
    def _(line):
        for part in range(2):
            diagonal = jnp.sum(jnp.where(eye, blocks[part, line], 0.0), axis=0, keepdims=True)
            pack[part, pl.ds(48 + line, 1), :] = diagonal

    for side, line in ((0, 0), (1, LINES - 1)):
        for part in range(2):
            pe_own[side, 8 * part : 8 * part + 8, :] = probes[part, pl.ds(q * OWNED * LINES + line, OWNED, stride=LINES), :]
            pe_own[side, 17 + part : 18 + part, :] = pack[part, 48 + line : 49 + line, :]
        pe_own[side, 16:17, :] = pack[0, 56 + line : 57 + line, :]

    pl.semaphore_wait(barrier, 5 + planes - 1 + 15)

    @pl.when(is_head)
    def _():
        for s in range(len(ORDER)):
            z_head(s).start()

    k_mirror.start()
    p_mirror.start()
    e_up.start()
    e_down.start()

    def prepare(w, probe_re, probe_im, weight, diag_re, diag_im):
        line = d * LINES + zh * (w - FIRST) + (1 - zh) * (SPAN - 1 - FIRST - w)
        inside = jnp.logical_and(line >= 0, line < doms * LINES)
        source_re = weight * probe_re
        source_im = weight * probe_im
        src[w, 0] = source_re
        src[w, 1] = source_im
        denom_re = table[0] * weight - diag_re
        denom_im = table[1] * weight - diag_im
        modulus = denom_re * denom_re + denom_im * denom_im
        inv_re[w] = jnp.where(inside, denom_re / modulus, 0.0)
        inv_im[w] = jnp.where(inside, -denom_im / modulus, 0.0)
        for j in range(NQ):
            g_re = inv_re[w, j : j + 1, :]
            g_im = inv_im[w, j : j + 1, :]
            y1r[w, 8 * j : 8 * j + 8, :] = source_re * g_re - source_im * g_im
            y1i[w, 8 * j : 8 * j + 8, :] = source_re * g_im + source_im * g_re

    def couple(w, ref, line):
        for position in range(6):
            row = zh * position + (1 - zh) * (5 - position)
            for part in range(2):
                cw[w, 6 * part + position : 6 * part + position + 1, :] = ref[part, pl.ds(row * LINES + line, 1), :]

    def prepare_packed(w, line, probe, packed):
        couple(w, packed, line)
        prepare(
            w,
            probe[0, pl.ds(line, OWNED, stride=LINES), :],
            probe[1, pl.ds(line, OWNED, stride=LINES), :],
            packed[0, pl.ds(56 + line, 1), :],
            packed[0, pl.ds(48 + line, 1), :],
            packed[1, pl.ds(48 + line, 1), :],
        )

    def prepare_edge(w, side):
        prepare(w, pe_in[side, 0:8, :], pe_in[side, 8:16, :], pe_in[side, 16:17, :], pe_in[side, 17:18, :], pe_in[side, 18:19, :])

    def own_line(w):
        return zh * (w - FIRST) + (1 - zh) * (SPAN - 1 - FIRST - w)

    def operand(w, block_re, block_im):
        re_high, re_low = split(jnp.where(eye, 0.0, block_re))
        im_high, im_low = split(jnp.where(eye, 0.0, block_im))
        for ref, re, im in ((rhi, re_high, im_high), (rlo, re_low, im_low)):
            ref[w - 3, 0:NY, 0:NY] = re
            ref[w - 3, 0:NY, NY:] = -im
            ref[w - 3, NY:, 0:NY] = im
            ref[w - 3, NY:, NY:] = re

    def image(yr, yi, w, into):
        into[...] = dot3(jnp.concatenate([yr[w], yi[w]], axis=1), rhi[w - 3], rlo[w - 3])

    def finish(yr, yi, w, image_ref, emit, order=range(NQ)):
        c_re = [cw[w, i : i + 1, :] for i in range(6)]
        c_im = [cw[w, 6 + i : 7 + i, :] for i in range(6)]
        source_re = src[w, 0]
        source_im = src[w, 1]
        for j in order:
            part = slice(8 * j, 8 * j + 8)
            a_re = image_ref[part, :NY] + source_re
            a_im = image_ref[part, NY:] + source_im
            for i, offset in enumerate(OFFSETS):
                n_re = yr[w + offset, part, :]
                n_im = yi[w + offset, part, :]
                a_re = a_re + (c_re[i] * n_re - c_im[i] * n_im)
                a_im = a_im + (c_re[i] * n_im + c_im[i] * n_re)
            g_re = inv_re[w, j : j + 1, :]
            g_im = inv_im[w, j : j + 1, :]
            emit(j, g_re * a_re - g_im * a_im, g_re * a_im + g_im * a_re)

    def keep(yr, yi, w):
        def emit(j, re, im):
            yr[w, 8 * j : 8 * j + 8, :] = re
            yi[w, 8 * j : 8 * j + 8, :] = im

        return emit

    def second(w, image_ref):
        finish(y1r, y1i, w, image_ref, keep(y2r, y2i, w))

    def third(w, image_ref):
        finish(y2r, y2i, w, image_ref, keep(y3r, y3i, w))

    def last(w, image_ref):
        line = own_line(w)
        field = {}

        def emit(j, re, im):
            field[j] = (re, im)

        finish(y3r, y3i, w, image_ref, emit, [a + 4 * b for a in range(4) for b in range(4)])
        sum_re = [None] * (2 * MOM)
        sum_im = [None] * (2 * MOM)
        for a in range(4):
            (r0, i0), (r1, i1), (r2, i2), (r3, i3) = (field[a + 4 * b] for b in range(4))
            er, ei, fr, fi = r0 + r2, i0 + i2, r0 - r2, i0 - i2
            gr, gi, hr, hi = r1 + r3, i1 + i3, r1 - r3, i1 - i3
            groups = ((er + gr, ei + gi), (fr - hi, fi + hr), (er - gr, ei - gi), (fr + hi, fi - hr))
            for k in range(2 * MOM):
                x_re, x_im = groups[(k + 1) % 4]
                w_re, w_im = WEIGHTS[k][a]
                t_re = w_re * x_re - w_im * x_im
                t_im = w_re * x_im + w_im * x_re
                sum_re[k] = t_re if a == 0 else sum_re[k] + t_re
                sum_im[k] = t_im if a == 0 else sum_im[k] + t_im
        for k in range(MOM):
            mom_ref[pl.ds(k * 16 + line, OWNED, stride=64), :] = sum_re[k]
            mom_ref[pl.ds(k * 16 + 8 + line, OWNED, stride=64), :] = sum_im[k]
        m_high, m_low = split(jnp.concatenate(sum_re + sum_im, axis=0))
        probe_lines = jnp.concatenate([probes[part, pl.ds(line, 64, stride=LINES), :] for part in range(2)], axis=0)
        gram[...] += dot3(probe_lines, m_high, m_low)

    def pairs(yr, yi, step, first, count):
        image(yr, yi, first, ima)

        @pl.loop(0, count // 2)
        def _(i):
            w = first + 2 * i
            image(yr, yi, w + 1, imb)
            step(w, ima)
            image(yr, yi, jnp.minimum(w + 2, first + count - 1), ima)
            step(w + 1, imb)

    def relay(s):
        z_copy(s).wait_recv()
        if ORDER[s] >= 2:
            y_copy(LINES - 1 - ORDER[s]).start()

        @pl.when(head == 0)
        def _():
            z_copy(s).start()

        if ORDER[s] < RIM:
            sz_copy(ORDER[s], c).start()

    def pass_small():
        k_mirror.wait_recv()
        y_pack().start()
        sz_pack(c).start()
        p_mirror.wait_recv()
        p_next.start()

    def prepare_z():
        sz_pack(o).wait_recv()
        e_down.wait_recv()
        e_up.wait_recv()

        @pl.loop(0, LINES)
        def _(t):
            prepare_packed(FIRST - 1 - t, (1 - zh) * t + zh * (LINES - 1 - t), pz, zk)

        prepare_edge(0, zh)

    def prepare_y():
        y_pack().wait_recv()
        sy_pack(c).start()
        p_next.wait_recv()
        sy_pack(o).wait_recv()

        @pl.loop(0, LINES)
        def _(u):
            prepare_packed(FIRST + LINES + u, (1 - zh) * (LINES - 1 - u) + zh * u, py, yk)

        prepare_edge(SPAN - 1, 1 - zh)

    gram[...] = jnp.zeros_like(gram)

    @pl.loop(FIRST, FIRST + LINES)
    def _(w):
        line = own_line(w)
        couple(w, pack, line)
        prepare(
            w,
            probes[0, pl.ds(q * OWNED * LINES + line, OWNED, stride=LINES), :],
            probes[1, pl.ds(q * OWNED * LINES + line, OWNED, stride=LINES), :],
            pack[0, pl.ds(56 + line, 1), :],
            pack[0, pl.ds(48 + line, 1), :],
            pack[1, pl.ds(48 + line, 1), :],
        )
        operand(w, blocks[0, line], blocks[1, line])

    @pl.when(far)
    def _():
        pass_small()
        prepare_z()
        pairs(y1r, y1i, second, FIRST, 4)

    relay(0)
    relay(1)
    pl.when(jnp.logical_not(far))(pass_small)
    relay(2)
    pl.when(jnp.logical_not(far))(prepare_z)
    relay(3)

    @pl.when(far)
    def _():
        prepare_y()

    @pl.when(jnp.logical_not(far))
    def _():
        pairs(y1r, y1i, second, FIRST, 2)

    relay(4)

    @pl.when(far)
    def _():
        pairs(y1r, y1i, second, FIRST + 4, 2)

    @pl.when(jnp.logical_not(far))
    def _():
        pairs(y1r, y1i, second, FIRST + 2, 2)

    relay(5)

    @pl.when(far)
    def _():
        pairs(y1r, y1i, second, FIRST + 6, 2)

    relay(6)
    relay(7)

    @pl.when(jnp.logical_not(far))
    def _():
        prepare_y()
        pairs(y1r, y1i, second, FIRST + 4, 4)

    @pl.loop(0, 3)
    def _(i):
        t = lax.rem(4 * i, RIM)
        w = FIRST - 1 - t
        sz_copy(t, o).wait_recv()
        operand(w, zb[0, t], zb[1, t])
        image(y1r, y1i, w, ima)
        sz_copy(t + 1, o).wait_recv()
        operand(w - 1, zb[0, t + 1], zb[1, t + 1])
        image(y1r, y1i, w - 1, imb)
        second(w, ima)
        second(w - 1, imb)

    y_copy(0).wait_recv()
    sy_copy(0, c).start()
    pairs(y2r, y2i, third, FIRST - 3, 8)
    pairs(y3r, y3i, last, FIRST, 2)

    @pl.loop(0, RIM)
    def _(u):
        @pl.when(u < RIM - 1)
        def _():
            y_copy(u + 1).wait_recv()
            sy_copy(u + 1, c).start()

        sy_copy(u, o).wait_recv()
        w = FIRST + LINES + u
        image(y3r, y3i, w - 6, imc)
        image(y2r, y2i, w - 3, imb)
        operand(w, yb[0, u], yb[1, u])
        image(y1r, y1i, w, ima)
        second(w, ima)
        third(w - 3, imb)
        last(w - 6, imc)

    lane = lax.broadcasted_iota(jnp.int32, (64, 128), 1)
    other = pltpu.roll(gram[64:, :], 64, 1)
    scale = 1.0 / float(doms * LINES * NY)
    partial = scale * (gram[:64, :] + jnp.where(lane < 64, other, -other))
    for i in range(planes):
        mine[i] = partial[i * rows : (i + 1) * rows, :]

    def dev(quad, dom):
        return {"quad": quad, "dom": dom}

    def plane_copy(i):
        to = lax.rem(m + i, planes)
        return pltpu.make_async_remote_copy(
            src_ref=mine.at[to], dst_ref=gathered.at[i], send_sem=s1.at[i], recv_sem=r1.at[i],
            device_id=dev(q, to * 2 + zh), device_id_type=pl.DeviceIdType.MESH,
        )

    def column_copy(i):
        to = lax.rem(slot + i, 16)
        return pltpu.make_async_remote_copy(
            src_ref=column.at[slot], dst_ref=column.at[slot], send_sem=s2.at[i], recv_sem=r2.at[i],
            device_id=dev(lax.rem(to, 8), 2 * m + lax.div(to, 8)), device_id_type=pl.DeviceIdType.MESH,
        )

    def column_arrived(i):
        come = lax.rem(slot + 16 - i, 16)
        return pltpu.make_async_remote_copy(
            src_ref=column.at[come], dst_ref=column.at[come], send_sem=s2.at[i], recv_sem=r2.at[i],
            device_id=dev(lax.rem(come, 8), 2 * m + lax.div(come, 8)), device_id_type=pl.DeviceIdType.MESH,
        )

    def full_copy(i):
        to = lax.rem(m + i, planes)
        return pltpu.make_async_remote_copy(
            src_ref=total, dst_ref=full.at[m], send_sem=s3.at[i], recv_sem=r3.at[i],
            device_id=dev(q, to * 2 + zh), device_id_type=pl.DeviceIdType.MESH,
        )

    def full_arrived(i):
        come = lax.rem(m + planes - i, planes)
        return pltpu.make_async_remote_copy(
            src_ref=total, dst_ref=full.at[come], send_sem=s3.at[i], recv_sem=r3.at[i],
            device_id=dev(q, come * 2 + zh), device_id_type=pl.DeviceIdType.MESH,
        )

    @pl.loop(1, planes)
    def _(i):
        plane_copy(i).start()

    gathered[0] = mine[m]

    @pl.loop(1, planes)
    def _(i):
        plane_copy(i).wait_recv()

    column[slot] = functools.reduce(lambda a, b: a + b, [gathered[i] for i in range(planes)])

    @pl.loop(1, 16)
    def _(i):
        column_copy(i).start()

    @pl.loop(1, 16)
    def _(i):
        column_arrived(i).wait_recv()

    group = lax.div(lax.broadcasted_iota(jnp.int32, (rows, NY), 1), 8)
    sums = [column[i] + column[8 + i] for i in range(8)]
    for pair in range(8):
        value = jnp.zeros((rows, NY), jnp.float32)
        for half in range(2):
            for i in range(8):
                to = 8 * half + i
                shift = (to - 2 * pair - half) % 16 * 8
                moved = pltpu.roll(sums[i], shift, 1) if shift else sums[i]
                value = jnp.where(group == to, moved, value)
        total[pair] = value

    @pl.loop(1, planes)
    def _(i):
        full_copy(i).start()

    full[m] = total[...]

    @pl.loop(1, planes)
    def _(i):
        full_arrived(i).wait_recv()

    for i in range(planes):
        for pair in range(8):
            value = full[i, pair]
            out_ref[2 * pair, rows * i : rows * (i + 1), :] = value[:, :64]
            out_ref[2 * pair + 1, rows * i : rows * (i + 1), :] = value[:, 64:]

    @pl.loop(1, planes)
    def _(i):
        plane_copy(i).wait_send()
        full_copy(i).wait_send()

    @pl.loop(1, 16)
    def _(i):
        column_copy(i).wait_send()

    k_mirror.wait_send()
    p_mirror.wait_send()
    p_next.wait_send()
    e_up.wait_send()
    e_down.wait_send()
    for s in range(len(ORDER)):
        z_copy(s).wait_send()
    y_pack().wait_send()
    sz_pack(c).wait_send()
    sy_pack(c).wait_send()
    for i in range(RIM):
        y_copy(i).wait_send()
        sz_copy(i, c).wait_send()
        sy_copy(i, c).wait_send()


def on_device(doms, probes, mass_weights, blocks, couplings):
    f32 = jnp.float32
    planes = doms // 2
    rows = 64 // planes
    vmem = pl.BlockSpec(memory_space=pltpu.VMEM)
    dma = pltpu.SemaphoreType.DMA
    moments, projected = pl.pallas_call(
        functools.partial(sweep_kernel, doms),
        out_shape=(jax.ShapeDtypeStruct((512, NY), f32), jax.ShapeDtypeStruct((16, 64, 64), f32)),
        in_specs=[pl.BlockSpec(memory_space=pl.ANY)] * 4,
        out_specs=(vmem, vmem),
        scratch_shapes=[
            pltpu.VMEM((2, 512, NY), f32),
            pltpu.VMEM((2, LINES, NY, NY), f32),
            pltpu.VMEM((2, NQ, NY), f32),
            pltpu.VMEM((2, LINES, NY, NY), f32),
            pltpu.VMEM((2, RIM, NY, NY), f32),
            pltpu.VMEM((2, 64, NY), f32),
            pltpu.VMEM((2, 64, NY), f32),
            pltpu.VMEM((2, 64, NY), f32),
            pltpu.VMEM((2, 64, NY), f32),
            pltpu.VMEM((2, 24, NY), f32),
            pltpu.VMEM((2, 24, NY), f32),
            pltpu.VMEM((2, 64, NY), f32),
            pltpu.VMEM((SPAN, NQ, NY), f32),
            pltpu.VMEM((SPAN, NQ, NY), f32),
            pltpu.VMEM((SPAN, 2, OWNED, NY), f32),
            pltpu.VMEM((SPAN, 16, NY), f32),
            pltpu.VMEM((20, 2 * NY, 2 * NY), jnp.bfloat16),
            pltpu.VMEM((20, 2 * NY, 2 * NY), jnp.bfloat16),
        ]
        + [pltpu.VMEM((SPAN, NQ * OWNED, NY), f32)] * 6
        + [pltpu.VMEM((NY, 2 * NY), f32)] * 3
        + [
            pltpu.VMEM((NY, NY), f32),
            pltpu.VMEM((planes, rows, NY), f32),
            pltpu.VMEM((planes, rows, NY), f32),
            pltpu.VMEM((16, rows, NY), f32),
            pltpu.VMEM((8, rows, NY), f32),
            pltpu.VMEM((planes, 8, rows, NY), f32),
        ]
        + [dma((5,))]
        + [dma((8,))] * 2
        + [dma((7,))] * 6
        + [dma((3,))] * 2
        + [dma((2,))] * 2
        + [dma((16,))] * 6,
        compiler_params=pltpu.CompilerParams(collective_id=0, has_side_effects=True, vmem_limit_bytes=60 * 1024 * 1024),
    )(probes.reshape(2, 512, NY), mass_weights, blocks, couplings.reshape(2, 48, NY))
    return moments.reshape(OWNED, MOM, 2, LINES, NY), projected.reshape(2, 8, 64, 64)


def solution(mesh):
    return jax.shard_map(
        functools.partial(on_device, mesh.shape["dom"]),
        mesh=mesh,
        in_specs=(P(None, None, "dom", None), P("dom", None), P(None, "dom", None, None), P(None, None, "dom", None)),
        out_specs=(P("quad", None, None, "dom", None), P()),
        check_vma=False,
    )
```

time: 89.6 us -> 67.7 us (0.76)
  local copies, waits for them, and re-layouts: 15.7 us -> 2.53 us
  Pallas kernels: 72.9 us -> 64.4 us
    pallas_call x1 -> x0, Pallas kernels: 20 us -> none  [on_device(): pl.pallas_call(functools.partial(reduce_kernel, planes), out_shape=jax.Sh...]
    pallas_call x1, Pallas kernels: 52.8 us -> 64.4 us  [on_device(): pl.pallas_call(functools.partial(sweep_kernel, doms), out_shape=(jax.Shap...]
    transpose x1 -> x0, local copies, waits for them, and re-layouts: 4.38 us -> none  [on_device(): full.reshape(planes, 8, rows, 2, 8, 8).transpose(3, 4, 0, 2, 1, 5)]
    reshape x1 -> x0, local copies, waits for them, and re-layouts: 3.94 us -> none  [on_device(): full.reshape(planes, 8, rows, 2, 8, 8).transpose(3, 4, 0, 2, 1, 5)]
    unnamed x13 -> x4, local copies, waits for them, and re-layouts: 5.77 us -> 2.53 us
    pallas_call x1 -> x0, local copies, waits for them, and re-layouts: 1.56 us -> none  [on_device(): pl.pallas_call(functools.partial(reduce_kernel, planes), out_shape=jax.Sh...]
where the time goes in v2:
time: 67.7 us; the launch traced here: 67.6 us
  Pallas kernels  64.4 us (95%)
  local copies, waits for them, and re-layouts  2.53 us (4%)
    pallas_call x1, Pallas kernels, on_device(): pl.pallas_call(functools.partial(sweep_kernel, doms), out_shape=(jax.Shap...  64.4 us
    unnamed x4, local copies, waits for them, and re-layouts  2.53 us

profile of v2, /device:TPU:1, one launch (start us, length us, event | category | flops | bytes accessed | tf_op | source)
XLA Modules:
  0.0 67.6 jit_solution(1058412000931154381)
XLA Ops:
  0.6 64.4 %shard_map.59 = (f32[512,128]{1,0:T(8,128)}, f32[16,64,64]{2,1,0:T(8,128)}) custom-call(f32[2,512,128]{2,1,0:T(8,128)} %bitcast.4, f32[8,128]{1,0:T(8,128)} %mass_hbm.1, f32[2,8,128,128]{3,2,1,0:T(8,128)} %blocks_hbm.1, f32[2,48,128]{2,1,0:T(8,128)} %bitcast.7), custom_call_target="tpu_custom_call" | custom-call | tf_op jit(solution)/shard_map/pallas_call | solution.py:572
  65.1 0.0 copy-start
  65.1 1.7 %copy.8 = f32[8,4,2,8,128]{4,3,2,1,0:T(8,128)} copy(f32[8,4,2,8,128]{4,3,2,1,0:T(8,128)} %bitcast.6) | data formatting | bytes 524288
  66.8 0.0 copy-done
  66.8 0.8 %copy.9 = f32[2,8,64,64]{3,2,1,0:T(8,128)} copy(f32[2,8,64,64]{3,2,1,0:T(8,128)S(1)} %bitcast.5) | data formatting | bytes 524288
Async XLA Ops:
  65.1 1.7 %copy-start = (f32[16,64,64]{2,1,0:T(8,128)S(1)}, f32[16,64,64]{2,1,0:T(8,128)}, u32[]{:S(2)}) copy-start(f32[16,64,64]{2,1,0:T(8,128)} %get-tuple-element.5) | copy-start | bytes 786436

commit v3 on v2

--- a/solution.py
+++ b/solution.py
@@ -20,6 +20,8 @@
 SPAN = 26
 ORDER = (7, 0, 6, 1, 5, 4, 3, 2)
 RIM = 6
+PLANE_ORDER = (10, 6, 9, 11, 14, 2, 8, 5, 7, 13, 3, 15, 1, 12, 4)
+COLUMN_ORDER = (8, 7, 9, 6, 10, 5, 11, 4, 12, 3, 13, 2, 14, 15, 1)
 NT = (((1,), (1,)), ((), ()))
 
 
@@ -116,13 +118,15 @@
         )
 
     def z_copy(s):
-        t = ORDER[s]
-        return copy(zb.at[c, t], zb.at[c, t], zs_send.at[s], zs_recv.at[s], q_to, d_to)
+        t = ORDER[s // 2]
+        piece = zb.at[c, t, pl.ds(s % 2 * 64, 64), :]
+        return copy(piece, piece, zs_send.at[s], zs_recv.at[s], q_to, d_to)
 
     def z_head(s):
-        t = ORDER[s]
+        t = ORDER[s // 2]
+        half = pl.ds(s % 2 * 64, 64)
         line = zh * t + (1 - zh) * (LINES - 1 - t)
-        return copy(blocks_hbm.at[c, line], zb.at[c, t], zs_send.at[s], zs_recv.at[s], q_to, d_to)
+        return copy(blocks_hbm.at[c, line, half, :], zb.at[c, t, half, :], zs_send.at[s], zs_recv.at[s], q_to, d_to)
 
     def y_pack():
         return copy(zk.at[c], yk.at[c], ys_send.at[RIM], ys_recv.at[RIM], q, y_to)
@@ -175,7 +179,7 @@
 
     @pl.when(is_head)
     def _():
-        for s in range(len(ORDER)):
+        for s in range(2 * len(ORDER)):
             z_head(s).start()
 
     k_mirror.start()
@@ -307,14 +311,16 @@
             image(yr, yi, jnp.minimum(w + 2, first + count - 1), ima)
             step(w + 1, imb)
 
+        if count % 2:
+            step(first + count - 1, ima)
+
     def relay(s):
-        z_copy(s).wait_recv()
+        for piece in (2 * s, 2 * s + 1):
+            z_copy(piece).wait_recv()
+            pl.when(head == 0)(z_copy(piece).start)
+
         if ORDER[s] >= 2:
             y_copy(LINES - 1 - ORDER[s]).start()
-
-        @pl.when(head == 0)
-        def _():
-            z_copy(s).start()
 
         if ORDER[s] < RIM:
             sz_copy(ORDER[s], c).start()
@@ -337,9 +343,11 @@
 
         prepare_edge(0, zh)
 
-    def prepare_y():
+    def share_y():
         y_pack().wait_recv()
         sy_pack(c).start()
+
+    def prepare_y():
         p_next.wait_recv()
         sy_pack(o).wait_recv()
 
@@ -365,54 +373,7 @@
         )
         operand(w, blocks[0, line], blocks[1, line])
 
-    @pl.when(far)
-    def _():
-        pass_small()
-        prepare_z()
-        pairs(y1r, y1i, second, FIRST, 4)
-
-    relay(0)
-    relay(1)
-    pl.when(jnp.logical_not(far))(pass_small)
-    relay(2)
-    pl.when(jnp.logical_not(far))(prepare_z)
-    relay(3)
-
-    @pl.when(far)
-    def _():
-        prepare_y()
-
-    @pl.when(jnp.logical_not(far))
-    def _():
-        pairs(y1r, y1i, second, FIRST, 2)
-
-    relay(4)
-
-    @pl.when(far)
-    def _():
-        pairs(y1r, y1i, second, FIRST + 4, 2)
-
-    @pl.when(jnp.logical_not(far))
-    def _():
-        pairs(y1r, y1i, second, FIRST + 2, 2)
-
-    relay(5)
-
-    @pl.when(far)
-    def _():
-        pairs(y1r, y1i, second, FIRST + 6, 2)
-
-    relay(6)
-    relay(7)
-
-    @pl.when(jnp.logical_not(far))
-    def _():
-        prepare_y()
-        pairs(y1r, y1i, second, FIRST + 4, 4)
-
-    @pl.loop(0, 3)
-    def _(i):
-        t = lax.rem(4 * i, RIM)
+    def z_pair(t):
         w = FIRST - 1 - t
         sz_copy(t, o).wait_recv()
         operand(w, zb[0, t], zb[1, t])
@@ -423,12 +384,99 @@
         second(w, ima)
         second(w - 1, imb)
 
-    y_copy(0).wait_recv()
-    sy_copy(0, c).start()
-    pairs(y2r, y2i, third, FIRST - 3, 8)
-    pairs(y3r, y3i, last, FIRST, 2)
-
-    @pl.loop(0, RIM)
+    def share(u):
+        y_copy(u).wait_recv()
+        sy_copy(u, c).start()
+
+    def y_line(u):
+        sy_copy(u, o).wait_recv()
+        w = FIRST + LINES + u
+        image(y2r, y2i, w - 3, imb)
+        operand(w, yb[0, u], yb[1, u])
+        image(y1r, y1i, w, ima)
+        second(w, ima)
+        third(w - 3, imb)
+
+    own = functools.partial(pairs, y1r, y1i, second)
+
+    @pl.when(jnp.logical_not(far))
+    def _():
+        for s in range(4):
+            relay(s)
+        pass_small()
+        relay(4)
+        prepare_z()
+        relay(5)
+        own(FIRST, 2)
+        relay(6)
+        own(FIRST + 2, 2)
+        relay(7)
+        share_y()
+        prepare_y()
+        own(FIRST + 4, 4)
+        for u in range(3):
+            share(u)
+        z_pair(0)
+        pairs(y2r, y2i, third, FIRST + 1, 4)
+        pl.loop(0, 2)(y_line)
+        z_pair(4)
+        y_line(2)
+
+    @pl.when(jnp.logical_and(far, head == 0))
+    def _():
+        pass_small()
+        for s in range(3):
+            relay(s)
+        prepare_z()
+        relay(3)
+        own(FIRST, 2)
+        relay(4)
+        own(FIRST + 2, 2)
+        relay(5)
+        share_y()
+        relay(6)
+        relay(7)
+        prepare_y()
+        share(0)
+        share(1)
+        own(FIRST + 4, 4)
+        z_pair(0)
+        share(2)
+        pairs(y2r, y2i, third, FIRST + 1, 4)
+        z_pair(4)
+        pl.loop(0, 3)(y_line)
+
+    @pl.when(is_head)
+    def _():
+        pass_small()
+        prepare_z()
+        own(FIRST, 4)
+        relay(0)
+        relay(1)
+        share_y()
+        relay(2)
+        prepare_y()
+        relay(3)
+        own(FIRST + 4, 4)
+        relay(4)
+        share(0)
+        z_pair(0)
+        relay(5)
+        pairs(y2r, y2i, third, FIRST + 1, 4)
+        relay(6)
+        share(1)
+        z_pair(4)
+        y_line(0)
+        relay(7)
+        share(2)
+        pl.loop(1, 3)(y_line)
+
+    share(3)
+    z_pair(2)
+    pairs(y2r, y2i, third, FIRST - 3, 4)
+    pairs(y3r, y3i, last, FIRST, 5)
+
+    @pl.loop(3, RIM)
     def _(u):
         @pl.when(u < RIM - 1)
         def _():
@@ -490,24 +538,20 @@
             device_id=dev(q, come * 2 + zh), device_id_type=pl.DeviceIdType.MESH,
         )
 
-    @pl.loop(1, planes)
-    def _(i):
+    for i in PLANE_ORDER:
         plane_copy(i).start()
 
     gathered[0] = mine[m]
 
-    @pl.loop(1, planes)
-    def _(i):
+    for i in range(1, planes):
         plane_copy(i).wait_recv()
 
     column[slot] = functools.reduce(lambda a, b: a + b, [gathered[i] for i in range(planes)])
 
-    @pl.loop(1, 16)
-    def _(i):
+    for i in COLUMN_ORDER:
         column_copy(i).start()
 
-    @pl.loop(1, 16)
-    def _(i):
+    for i in range(1, 16):
         column_arrived(i).wait_recv()
 
     group = lax.div(lax.broadcasted_iota(jnp.int32, (rows, NY), 1), 8)
@@ -522,14 +566,12 @@
                 value = jnp.where(group == to, moved, value)
         total[pair] = value
 
-    @pl.loop(1, planes)
-    def _(i):
+    for i in PLANE_ORDER:
         full_copy(i).start()
 
     full[m] = total[...]
 
-    @pl.loop(1, planes)
-    def _(i):
+    for i in range(1, planes):
         full_arrived(i).wait_recv()
 
     for i in range(planes):
@@ -552,7 +594,7 @@
     p_next.wait_send()
     e_up.wait_send()
     e_down.wait_send()
-    for s in range(len(ORDER)):
+    for s in range(2 * len(ORDER)):
         z_copy(s).wait_send()
     y_pack().wait_send()
     sz_pack(c).wait_send()
@@ -605,7 +647,7 @@
             pltpu.VMEM((planes, 8, rows, NY), f32),
         ]
         + [dma((5,))]
-        + [dma((8,))] * 2
+        + [dma((16,))] * 2
         + [dma((7,))] * 6
         + [dma((3,))] * 2
         + [dma((2,))] * 2

time: 67.7 us -> 64.8 us (0.957)
  Pallas kernels: 64.4 us -> 61.5 us
    pallas_call x1, Pallas kernels: 64.4 us -> 61.5 us  [on_device(): pl.pallas_call(functools.partial(sweep_kernel, doms), out_shape=(jax.Shap...]
where the time goes in v3:
time: 64.8 us; the launch traced here: 64.7 us
  Pallas kernels  61.5 us (95%)
  local copies, waits for them, and re-layouts  2.53 us (4%)
  between operations  0.65 us (1%)
    pallas_call x1, Pallas kernels, on_device(): pl.pallas_call(functools.partial(sweep_kernel, doms), out_shape=(jax.Shap...  61.5 us
    unnamed x4, local copies, waits for them, and re-layouts  2.53 us

profile of v3, /device:TPU:1, one launch (start us, length us, event | category | flops | bytes accessed | tf_op | source)
XLA Modules:
  0.0 64.7 jit_solution(8860342611112199426)
XLA Ops:
  0.6 61.5 %shard_map.59 = (f32[512,128]{1,0:T(8,128)}, f32[16,64,64]{2,1,0:T(8,128)}) custom-call(f32[2,512,128]{2,1,0:T(8,128)} %bitcast.4, f32[8,128]{1,0:T(8,128)} %mass_hbm.1, f32[2,8,128,128]{3,2,1,0:T(8,128)} %blocks_hbm.1, f32[2,48,128]{2,1,0:T(8,128)} %bitcast.7), custom_call_target="tpu_custom_call" | custom-call | tf_op jit(solution)/shard_map/pallas_call | solution.py:614
  62.2 0.0 copy-start
  62.2 1.7 %copy.8 = f32[8,4,2,8,128]{4,3,2,1,0:T(8,128)} copy(f32[8,4,2,8,128]{4,3,2,1,0:T(8,128)} %bitcast.6) | data formatting | bytes 524288
  63.9 0.0 copy-done
  63.9 0.8 %copy.9 = f32[2,8,64,64]{3,2,1,0:T(8,128)} copy(f32[2,8,64,64]{3,2,1,0:T(8,128)S(1)} %bitcast.5) | data formatting | bytes 524288
Async XLA Ops:
  62.2 1.7 %copy-start = (f32[16,64,64]{2,1,0:T(8,128)S(1)}, f32[16,64,64]{2,1,0:T(8,128)}, u32[]{:S(2)}) copy-start(f32[16,64,64]{2,1,0:T(8,128)} %get-tuple-element.5) | copy-start | bytes 786436

commit v4 on v3

--- a/solution.py
+++ b/solution.py
@@ -51,7 +51,7 @@
     doms, probes_hbm, mass_hbm, blocks_hbm, coup_hbm, mom_ref, out_ref,
     probes, blocks, table, zb, yb, zk, yk, pz, py, pe_own, pe_in, pack, inv_re, inv_im, src, cw, rhi, rlo,
     y1r, y1i, y2r, y2i, y3r, y3i, ima, imb, imc, gram, mine, gathered, column, total, full,
-    in_sem, zs_send, zs_recv, ys_send, ys_recv, sz_send, sz_recv, sy_send, sy_recv, ps_send, ps_recv, es_send, es_recv,
+    in_sem, zs_send, zs_recv, zk_send, ys_send, ys_recv, sz_send, sz_recv, sy_send, sy_recv, ps_send, ps_recv, es_send, es_recv,
     s1, r1, s2, r2, s3, r3,
 ):
     q = lax.axis_index("quad")
@@ -67,15 +67,14 @@
     at_top = lax.div(q + 2, 8)
     at_bottom = 1 - lax.div(q + 6, 8)
     head = (1 - c) * at_top + c * at_bottom
-    tail = (1 - c) * at_bottom + c * at_top
     q_to = lax.rem(q + 8 + 2 - 4 * c, 8)
-    q_from = lax.rem(q + 8 - 2 + 4 * c, 8)
     d_to = d + head * (1 - 2 * zh)
-    d_from = d + tail * (1 - 2 * zh)
     sib = q + 1 - 2 * c
     mirror = 2 * (3 - zl) + c
     is_head = head == 1
-    far = lax.div(c * (3 - zl) + (1 - c) * zl, 2) == 1
+    depth = c * (3 - zl) + (1 - c) * zl
+    far = lax.div(depth, 2) == 1
+    q_skip = lax.rem(q + 8 + 4 - 8 * c, 8)
     planes = doms // 2
     rows = 64 // planes
     m = lax.div(d, 2)
@@ -96,12 +95,6 @@
     def greet(quad, dom):
         pl.semaphore_signal(barrier, inc=1, device_id={"quad": quad, "dom": dom}, device_id_type=pl.DeviceIdType.MESH)
 
-    greet(mirror, flip)
-    greet(q_from, d_from)
-    greet(q, up)
-    greet(q, down)
-    greet(sib, d)
-
     @pl.loop(1, planes)
     def _(i):
         greet(q, lax.rem(m + i, planes) * 2 + zh)
@@ -121,6 +114,11 @@
         t = ORDER[s // 2]
         piece = zb.at[c, t, pl.ds(s % 2 * 64, 64), :]
         return copy(piece, piece, zs_send.at[s], zs_recv.at[s], q_to, d_to)
+
+    def z_skip(s):
+        t = ORDER[s // 2]
+        piece = zb.at[c, t, pl.ds(s % 2 * 64, 64), :]
+        return copy(piece, piece, zk_send.at[s], zs_recv.at[s], q_skip, d)
 
     def z_head(s):
         t = ORDER[s // 2]
@@ -175,7 +173,7 @@
             pe_own[side, 17 + part : 18 + part, :] = pack[part, 48 + line : 49 + line, :]
         pe_own[side, 16:17, :] = pack[0, 56 + line : 57 + line, :]
 
-    pl.semaphore_wait(barrier, 5 + planes - 1 + 15)
+    pl.semaphore_wait(barrier, planes - 1 + 15)
 
     @pl.when(is_head)
     def _():
@@ -317,7 +315,14 @@
     def relay(s):
         for piece in (2 * s, 2 * s + 1):
             z_copy(piece).wait_recv()
-            pl.when(head == 0)(z_copy(piece).start)
+            first = z_skip(piece), z_copy(piece)
+
+            @pl.when(depth == 0)
+            def _():
+                first[0].start()
+                first[1].start()
+
+            pl.when(depth == 2)(first[1].start)
 
         if ORDER[s] >= 2:
             y_copy(LINES - 1 - ORDER[s]).start()
@@ -594,8 +599,17 @@
     p_next.wait_send()
     e_up.wait_send()
     e_down.wait_send()
-    for s in range(2 * len(ORDER)):
-        z_copy(s).wait_send()
+
+    @pl.when(depth != 1)
+    def _():
+        for s in range(2 * len(ORDER)):
+            z_copy(s).wait_send()
+
+    @pl.when(depth == 0)
+    def _():
+        for s in range(2 * len(ORDER)):
+            z_skip(s).wait_send()
+
     y_pack().wait_send()
     sz_pack(c).wait_send()
     sy_pack(c).wait_send()
@@ -613,7 +627,7 @@
     dma = pltpu.SemaphoreType.DMA
     moments, projected = pl.pallas_call(
         functools.partial(sweep_kernel, doms),
-        out_shape=(jax.ShapeDtypeStruct((512, NY), f32), jax.ShapeDtypeStruct((16, 64, 64), f32)),
+        out_shape=(pltpu.VMEM((512, NY), f32), pltpu.VMEM((16, 64, 64), f32)),
         in_specs=[pl.BlockSpec(memory_space=pl.ANY)] * 4,
         out_specs=(vmem, vmem),
         scratch_shapes=[
@@ -647,7 +661,7 @@
             pltpu.VMEM((planes, 8, rows, NY), f32),
         ]
         + [dma((5,))]
-        + [dma((16,))] * 2
+        + [dma((16,))] * 3
         + [dma((7,))] * 6
         + [dma((3,))] * 2
         + [dma((2,))] * 2

time: 64.8 us -> 63.7 us (0.983)
  local copies, waits for them, and re-layouts: 2.53 us -> 1.5 us
    unnamed x4 -> x2, local copies, waits for them, and re-layouts: 2.53 us -> 1.5 us
where the time goes in v4:
time: 63.7 us; the launch traced here: 63.6 us
  Pallas kernels  61.5 us (97%)
  local copies, waits for them, and re-layouts  1.5 us (2%)
  between operations  0.64 us (1%)
    pallas_call x1, Pallas kernels, on_device(): pl.pallas_call(functools.partial(sweep_kernel, doms), out_shape=(pltpu.VM...  61.5 us
    unnamed x2, local copies, waits for them, and re-layouts  1.5 us

profile of v4, /device:TPU:1, one launch (start us, length us, event | category | flops | bytes accessed | tf_op | source)
XLA Modules:
  0.0 63.6 jit_solution(9843744936148391393)
XLA Ops:
  0.6 61.5 %shard_map.59 = (f32[512,128]{1,0:T(8,128)S(1)}, f32[16,64,64]{2,1,0:T(8,128)S(1)}) custom-call(f32[2,512,128]{2,1,0:T(8,128)} %bitcast.6, f32[8,128]{1,0:T(8,128)} %mass_hbm.1, f32[2,8,128,128]{3,2,1,0:T(8,128)} %blocks_hbm.1, f32[2,48,128]{2,1,0:T(8,128)} %bitcast.7), custom_call_target="tpu_custom_call" | custom-call | tf_op jit(solution)/shard_map/pallas_call | solution.py:628
  62.1 0.7 %copy.8 = f32[8,4,2,8,128]{4,3,2,1,0:T(8,128)} copy(f32[8,4,2,8,128]{4,3,2,1,0:T(8,128)S(1)} %bitcast.5) | data formatting | bytes 524288
  62.8 0.8 %copy.9 = f32[2,8,64,64]{3,2,1,0:T(8,128)} copy(f32[2,8,64,64]{3,2,1,0:T(8,128)S(1)} %bitcast.4) | data formatting | bytes 524288

commit v5 on v4

--- a/solution.py
+++ b/solution.py
@@ -424,14 +424,17 @@
         z_pair(0)
         pairs(y2r, y2i, third, FIRST + 1, 4)
         pl.loop(0, 2)(y_line)
+        for u in range(3, RIM):
+            share(u)
         z_pair(4)
         y_line(2)
 
     @pl.when(jnp.logical_and(far, head == 0))
     def _():
+        relay(0)
+        relay(1)
         pass_small()
-        for s in range(3):
-            relay(s)
+        relay(2)
         prepare_z()
         relay(3)
         own(FIRST, 2)
@@ -476,14 +479,14 @@
         share(2)
         pl.loop(1, 3)(y_line)
 
-    share(3)
+    pl.when(far)(functools.partial(share, 3))
     z_pair(2)
     pairs(y2r, y2i, third, FIRST - 3, 4)
     pairs(y3r, y3i, last, FIRST, 5)
 
     @pl.loop(3, RIM)
     def _(u):
-        @pl.when(u < RIM - 1)
+        @pl.when(jnp.logical_and(far, u < RIM - 1))
         def _():
             y_copy(u + 1).wait_recv()
             sy_copy(u + 1, c).start()
@@ -532,14 +535,13 @@
     def full_copy(i):
         to = lax.rem(m + i, planes)
         return pltpu.make_async_remote_copy(
-            src_ref=total, dst_ref=full.at[m], send_sem=s3.at[i], recv_sem=r3.at[i],
+            src_ref=total, dst_ref=full.at[m], send_sem=s3.at[i], recv_sem=r3.at[m],
             device_id=dev(q, to * 2 + zh), device_id_type=pl.DeviceIdType.MESH,
         )
 
-    def full_arrived(i):
-        come = lax.rem(m + planes - i, planes)
+    def full_arrived(come):
         return pltpu.make_async_remote_copy(
-            src_ref=total, dst_ref=full.at[come], send_sem=s3.at[i], recv_sem=r3.at[i],
+            src_ref=total, dst_ref=full.at[come], send_sem=s3.at[come], recv_sem=r3.at[come],
             device_id=dev(q, come * 2 + zh), device_id_type=pl.DeviceIdType.MESH,
         )
 
@@ -576,10 +578,8 @@
 
     full[m] = total[...]
 
-    for i in range(1, planes):
-        full_arrived(i).wait_recv()
-
     for i in range(planes):
+        pl.when(m != i)(full_arrived(i).wait_recv)
         for pair in range(8):
             value = full[i, pair]
             out_ref[2 * pair, rows * i : rows * (i + 1), :] = value[:, :64]

time: 63.7 us -> 63.8 us (level)
  no operation moved by 1% of the time
where the time goes in v5:
time: 63.8 us; the launch traced here: 63.7 us
  Pallas kernels  61.6 us (97%)
  local copies, waits for them, and re-layouts  1.5 us (2%)
  between operations  0.64 us (1%)
    pallas_call x1, Pallas kernels, on_device(): pl.pallas_call(functools.partial(sweep_kernel, doms), out_shape=(pltpu.VM...  61.6 us
    unnamed x2, local copies, waits for them, and re-layouts  1.5 us

profile of v5, /device:TPU:1, one launch (start us, length us, event | category | flops | bytes accessed | tf_op | source)
XLA Modules:
  0.0 63.7 jit_solution(7801799538149766731)
XLA Ops:
  0.6 61.6 %shard_map.59 = (f32[512,128]{1,0:T(8,128)S(1)}, f32[16,64,64]{2,1,0:T(8,128)S(1)}) custom-call(f32[2,512,128]{2,1,0:T(8,128)} %bitcast.6, f32[8,128]{1,0:T(8,128)} %mass_hbm.1, f32[2,8,128,128]{3,2,1,0:T(8,128)} %blocks_hbm.1, f32[2,48,128]{2,1,0:T(8,128)} %bitcast.7), custom_call_target="tpu_custom_call" | custom-call | tf_op jit(solution)/shard_map/pallas_call | solution.py:628
  62.2 0.7 %copy.8 = f32[8,4,2,8,128]{4,3,2,1,0:T(8,128)} copy(f32[8,4,2,8,128]{4,3,2,1,0:T(8,128)S(1)} %bitcast.5) | data formatting | bytes 524288
  62.9 0.8 %copy.9 = f32[2,8,64,64]{3,2,1,0:T(8,128)} copy(f32[2,8,64,64]{3,2,1,0:T(8,128)S(1)} %bitcast.4) | data formatting | bytes 524288
